TPU v7x, 32 devices: a whole 2x2x4 slice. The times are simulated.
32 devices in a mesh: island: 4 (over y, x), fsdp: 8 (over z, core).
Axes of the slice: x: 2, y: 2, z: 4, core: 2. Of those that a mesh axis runs over, the one named last changes fastest.
Arguments:
- weights: bfloat16 [4096, 14336], P(None, 'fsdp'), may hold values from -3 to 3
- momentum: bfloat16 [4096, 14336], P(None, 'fsdp'), may hold values from -0.59765625 to 0.59765625
- table: bfloat16 [2048, 4096], P(None, 'fsdp'), may hold values from -6 to 6
- token_ids: int32 [4, 2, 896], P('island'), may hold values from 0 to 2047
- cotangent: bfloat16 [4, 2, 896, 14336], P('island', None, None, 'fsdp'), may hold values from -6 to 6
Outputs:
- new_weights: bfloat16 [4096, 14336], P(None, 'fsdp')
All inputs are finite; a program needn't handle non-finite values.
Results may differ from a plain program's by a relative error of at most 0.005.
Values may be sent and summed in bfloat16 or wider, within the bound.
A program may use at most 128 MiB of HBM per device.

v0:
```python
import math

import jax
import jax.numpy as jnp
from jax import lax
from jax.sharding import PartitionSpec as P

beta_one = 0.9
beta_two = 0.95
adam_eps = 0.0001
inner_rate = 0.1
decay_rate = 0.1
outer_rate = 0.7
outer_moment = 0.9


def silu_slope(hidden):
    sigma = jax.nn.sigmoid(hidden)
    return sigma * (1.0 + hidden * (1.0 - sigma))


def grad_rows(inputs, upstream):
    return lax.dot_general(
        inputs, upstream, (((0,), (0,)), ((), ())), preferred_element_type=jnp.float32
    )


def make_upstream(hidden, island_cot):
    return (island_cot.astype(jnp.float32) * silu_slope(hidden) / island_cot.shape[0]).astype(
        jnp.bfloat16
    )


def inner_grad(x_local, work, island_cot, scale):
    whole = lax.all_gather(x_local, "fsdp", axis=1, tiled=True)
    hidden = jnp.dot(whole, work, preferred_element_type=jnp.float32) * scale
    upstream = make_upstream(hidden, island_cot)
    return grad_rows(whole, upstream) * scale


def outer_update(base, prior, mean):
    moment = outer_moment * prior.astype(jnp.float32) + mean
    return (base - outer_rate * (mean + outer_moment * moment)).astype(jnp.bfloat16)


def body(weights, momentum, table, token_ids, cotangent):
    scale = 1.0 / math.sqrt(weights.shape[0])
    start = weights.astype(jnp.float32)
    local = start
    first = jnp.zeros(start.shape, jnp.float32)
    second = jnp.zeros(start.shape, jnp.float32)
    for step in range(token_ids.shape[1]):
        work = weights if step == 0 else local.astype(jnp.bfloat16)
        x_local = jnp.take(table, token_ids[0, step], axis=0)
        grad = inner_grad(x_local, work, cotangent[0, step], scale)
        first = beta_one * first + (1.0 - beta_one) * grad
        second = beta_two * second + (1.0 - beta_two) * grad * grad
        m_hat = first / (1.0 - beta_one ** (step + 1))
        v_hat = second / (1.0 - beta_two ** (step + 1))
        local = local - inner_rate * (m_hat / (jnp.sqrt(v_hat) + adam_eps) + decay_rate * local)
    delta = (start - local).astype(jnp.bfloat16).astype(jnp.float32)
    islands = lax.axis_size("island")
    total = lax.psum(delta.astype(jnp.bfloat16), "island").astype(jnp.float32)
    return outer_update(start, momentum, total / islands)


def solution(mesh):
    placed = (
        P(None, "fsdp"),
        P(None, "fsdp"),
        P(None, "fsdp"),
        P("island", None, None),
        P("island", None, None, "fsdp"),
    )
    return jax.shard_map(
        body, mesh=mesh, in_specs=placed, out_specs=P(None, "fsdp"), check_vma=False
    )
```

profile of v0, /device:TPU:0, one launch (start us, length us, event | category | flops | bytes accessed | tf_op | source)
XLA Modules:
  0.0 570.0 jit_solution(5940361595412379827)
XLA Ops:
  6.5 0.0 copy-start
  6.5 0.0 all-gather.3.cloned.1.call-start
  6.5 0.9 slice_reduce_fusion
  7.5 0.7 copy-done
  8.2 3.5 gather_fusion
  11.7 1.1 broadcast_select_fusion.1
  12.8 0.0 all-gather.3.cloned.1.call-update
  12.8 0.0 all-gather.5.cloned.1.call-start
  12.9 3.5 gather_fusion.1
  16.4 1.2 broadcast_select_fusion
  17.6 0.0 all-gather.5.cloned.1.call-update
  17.6 0.0 all-reduce.2.cloned.1.call-start
  17.7 71.4 %all-gather.3.cloned.1.call-done = bf16[896,4096]{1,0:T(8,128)(2,1)} async-done(((bf16[896,512]{1,0:T(8,128)(2,1)}), bf16[896,4096]{1,0:T(8,128)(2,1)}) %all-gather.3.cloned.1.call-update) | async-done | bytes 7340048 | tf_op jit(solution)/shard_map/all_gather | solution.py:35
  89.0 0.0 copy-start.2
  89.0 21.6 %fusion.9 = bf16[896,1792]{1,0:T(8,128)(2,1)S(1)} fusion(bf16[896,4096]{1,0:T(8,128)(2,1)} %all-gather.3.cloned.1.call-done, bf16[4096,1792]{1,0:T(8,128)(2,1)} %param.7, bf16[1,2,896,1792]{3,2,1,0:T(8,128)(2,1)} %param.11), kind=kOutput, calls=%fused_computation.18 | convolution fusion | flops 13172604928 | bytes 28442624 | tf_op jit(solution)/shard_map/dot_general | solution.py:36
  110.7 0.0 copy-done.2
  110.7 19.1 %fusion.26 = f32[4096,1792]{1,0:T(8,128)} fusion(bf16[896,4096]{1,0:T(8,128)(2,1)S(1)} %copy-done.2, bf16[896,1792]{1,0:T(8,128)(2,1)S(1)} %fusion.9), kind=kOutput, calls=%fused_computation.36 | convolution fusion | flops 13153337344 | bytes 39911424 | tf_op jit(solution)/shard_map/dot_general | solution.py:23
  129.8 32.9 %all-gather.5.cloned.1.call-done = bf16[896,4096]{1,0:T(8,128)(2,1)} async-done(((bf16[896,512]{1,0:T(8,128)(2,1)}), bf16[896,4096]{1,0:T(8,128)(2,1)}) %all-gather.5.cloned.1.call-update) | async-done | bytes 7340048 | tf_op jit(solution)/shard_map/all_gather | solution.py:35
  162.7 39.3 %fusion.7.clone.4 = bf16[896,1792]{1,0:T(8,128)(2,1)} fusion(bf16[896,4096]{1,0:T(8,128)(2,1)} %all-gather.5.cloned.1.call-done, f32[4096,1792]{1,0:T(8,128)} %fusion.26, bf16[4096,1792]{1,0:T(8,128)(2,1)} %param.7, bf16[1,2,896,1792]{3,2,1,0:T(8,128)(2,1)} %param.11), kind=kOutput, calls=%fused_computation.15.clone.clone.clone.1 | convolution fusion | flops 13260685312 | bytes 57802752 | tf_op jit(solution)/shard_map/dot_general | solution.py:36
  202.0 65.5 %fusion.2 = bf16[4096,1792]{1,0:T(8,128)(2,1)} fusion(bf16[4096,1792]{1,0:T(8,128)(2,1)} %param.7, f32[4096,1792]{1,0:T(8,128)} %fusion.26, bf16[896,4096]{1,0:T(8,128)(2,1)} %all-gather.5.cloned.1.call-done, bf16[896,1792]{1,0:T(8,128)(2,1)} %fusion.7.clone.4), kind=kOutput, calls=%fused_computation.8 | convolution fusion | flops 13366198272 | bytes 69271552 | tf_op jit(solution)/shard_map/dot_general | solution.py:23
  267.5 0.0 all-reduce.2.cloned.1.call-update
  267.5 272.5 %all-reduce.2.cloned.1.call-done = bf16[4096,1792]{1,0:T(8,128)(2,1)} async-done(((bf16[4096,1792]{1,0:T(8,128)(2,1)}), bf16[4096,1792]{1,0:T(8,128)(2,1)}) %all-reduce.2.cloned.1.call-update) | async-done | bytes 14680080 | tf_op jit(solution)/shard_map/psum | solution.py:63
  540.0 0.0 copy-start.1
  540.0 23.5 %fusion.3 = bf16[4096,1792]{1,0:T(8,128)(2,1)} fusion(bf16[4096,1792]{1,0:T(8,128)(2,1)} %param.7, bf16[4096,1792]{1,0:T(8,128)(2,1)} %param.8, bf16[4096,1792]{1,0:T(8,128)(2,1)} %all-reduce.2.cloned.1.call-done), kind=kLoop, calls=%fused_computation.9 | loop fusion | flops 80740352 | bytes 58720256 | tf_op jit(solution)/shard_map/convert_element_type | solution.py:43
  563.5 0.0 copy-done.1
  (6 shorter events, 0.0 us)
Async XLA Ops:
  6.5 1.6 copy-start
  6.5 82.5 %all-gather.3.cloned.1.call-start = ((), (), s32[]{:S(2)}) async-start(), calls=%async_computation | async-start | bytes 8257536 | tf_op jit(solution)/shard_map/all_gather | solution.py:35
  12.8 149.9 %all-gather.5.cloned.1.call-start = ((), (), s32[]{:S(2)}) async-start(), calls=%async_computation.1 | async-start | bytes 8257536 | tf_op jit(solution)/shard_map/all_gather | solution.py:35
  17.6 522.4 %all-reduce.2.cloned.1.call-start = ((), (), s32[]{:S(2)}) async-start(), calls=%async_computation.2 | async-start | bytes 29360128 | tf_op jit(solution)/shard_map/psum | solution.py:63
  89.0 21.6 %copy-start.2 = (bf16[896,4096]{1,0:T(8,128)(2,1)S(1)}, bf16[896,4096]{1,0:T(8,128)(2,1)}, u32[]{:S(2)}) copy-start(bf16[896,4096]{1,0:T(8,128)(2,1)} %all-gather.3.cloned.1.call-done) | copy-start | bytes 22020100
  540.0 23.5 %copy-start.1 = (bf16[2048,512]{1,0:T(8,128)(2,1)S(1)}, bf16[2048,512]{1,0:T(8,128)(2,1)}, u32[]{:S(2)}) copy-start(bf16[2048,512]{1,0:T(8,128)(2,1)} %param.9) | copy-start | bytes 6291460
Sparse Core Ops, SparseCore 0:
  12.9 76.0 all-gather.2
  90.6 71.9 all-gather.4
  267.7 272.2 all-reduce.1
where the time goes:
time: 570 us
  waiting for transfers between devices  377 us (66%)
  matrix products  146 us (26%)
  other arithmetic  25.8 us (5%)
  between operations  13.2 us (2%)
  local copies, waits for them, and re-layouts  8.6 us (2%)
    psum x1, waiting for transfers between devices, body(): total = lax.psum(delta.astype(jnp.bfloat16), 'island').astype(jnp.float32)  272 us
    all_gather x2, waiting for transfers between devices, inner_grad(): whole = lax.all_gather(x_local, 'fsdp', axis=1, tiled=True)  104 us
    dot_general x2, matrix products, grad_rows(): lax.dot_general(inputs, upstream, (((0,), (0,)), ((), ())), preferred_ele...  84.7 us
    dot_general x2, matrix products, inner_grad(): hidden = jnp.dot(whole, work, preferred_element_type=jnp.float32) * scale  60.9 us
    convert_element_type x1, other arithmetic, outer_update(): (base - outer_rate * (mean + outer_moment * moment)).astype(jnp.bfloat16)  23.5 us
  transfers between devices with their start and end apart: 3, of which 3 were waited for; matrix products, arithmetic and copies ran while one was open for 8% of the time, Pallas kernels for 0%

commit v1 on v0

v1 whole, which is shorter than its diff:
```python
import functools
import math

import jax
import jax.numpy as jnp
from jax import lax
from jax.experimental import pallas as pl
from jax.experimental.pallas import tpu as pltpu
from jax.sharding import PartitionSpec as P

beta_one = 0.9
beta_two = 0.95
adam_eps = 0.0001
inner_rate = 0.1
decay_rate = 0.1
outer_rate = 0.7
outer_moment = 0.9

CHUNKS = 8


def silu_slope(hidden):
    sigma = jax.nn.sigmoid(hidden)
    return sigma * (1.0 + hidden * (1.0 - sigma))


def first_move(grad):
    return grad / (jnp.abs(grad) + adam_eps)


def second_move(grad_one, grad_two):
    first = beta_one * (1.0 - beta_one) * grad_one + (1.0 - beta_one) * grad_two
    second = (
        beta_two * (1.0 - beta_two) * grad_one * grad_one
        + (1.0 - beta_two) * grad_two * grad_two
    )
    m_hat = first * (1.0 / (1.0 - beta_one**2))
    v_hat = second * (1.0 / (1.0 - beta_two**2))
    return m_hat / (jnp.sqrt(v_hat) + adam_eps)


def step_kernel(step, shape, side, ids, pieces, weights, *refs):
    tiles, tok, scale = shape
    if step == 0:
        cot_own, cot_other, out, picks, turned, hidden, upstream = refs
    else:
        grad_one, cot_own, cot_other, out, picks, turned, hidden, upstream = refs
    at = pl.program_id(0)
    feat = pieces.shape[-1]
    rows = picks.shape[1]
    keep = 1.0 - inner_rate * decay_rate

    @pl.when(at == 0)
    def _():
        hidden[...] = jnp.zeros_like(hidden)

        @pl.loop(0, 2 * tok // 128)
        def _(part):
            span = pl.ds(pl.multiple_of(part * 128, 128), 128)
            row = lax.broadcasted_iota(jnp.int32, (128, rows), 1)
            picks[span, :] = (row == ids[span, :]).astype(jnp.float32).astype(jnp.bfloat16)

    @pl.when(at < tiles)
    def _():
        table = pieces[...].reshape(rows, feat)
        base = weights[...]
        place = pl.ds(pl.multiple_of(at * feat, feat), feat)
        for island in range(2):
            span = pl.ds(island * tok, tok)
            chosen = jnp.dot(
                picks[span, :], table, preferred_element_type=jnp.float32
            ).astype(jnp.bfloat16)
            turned[place, span] = chosen.T
            if step == 0:
                work = base
            else:
                moved = first_move(grad_one[island].astype(jnp.float32))
                work = (keep * base.astype(jnp.float32) - inner_rate * moved).astype(jnp.bfloat16)
            hidden[span, :] += jnp.dot(chosen, work, preferred_element_type=jnp.float32)

    @pl.when(at == tiles - 1)
    def _():
        for island, cot in enumerate((cot_own, cot_other)):

            @pl.loop(0, tok // 128)
            def _(part):
                inner = pl.ds(pl.multiple_of(part * 128, 128), 128)
                span = pl.ds(pl.multiple_of(island * tok + part * 128, 128), 128)
                value = cot[inner, :].astype(jnp.float32) * silu_slope(hidden[span, :] * scale)
                upstream[span, :] = (value * (1.0 / tok)).astype(jnp.bfloat16)

    @pl.when(at >= tiles)
    def _():
        place = pl.ds(pl.multiple_of((at - tiles) * feat, feat), feat)
        grads = [
            jnp.dot(
                turned[place, pl.ds(island * tok, tok)],
                upstream[pl.ds(island * tok, tok), :],
                preferred_element_type=jnp.float32,
            )
            * scale
            for island in range(2)
        ]
        if step == 0:
            for island in range(2):
                out[island] = grads[island].astype(jnp.bfloat16)
        else:
            total = (2.0 * (1.0 - keep * keep)) * weights[...].astype(jnp.float32)
            for island in range(2):
                one = grad_one[island].astype(jnp.float32)
                total += (keep * inner_rate) * first_move(one)
                total += inner_rate * second_move(one, grads[island])
            out[...] = total.astype(jnp.bfloat16)


def take_half(array, which, half):
    return lax.dynamic_slice_in_dim(array, which * half, half, array.ndim - 1)


def inner_step(step, side, ids, pieces, weights, grad_one, cot, cot_other):
    groups, tiles, quarter, feat = pieces.shape
    tok, half = cot_other.shape[1:]
    depth = weights.shape[0]
    rows = groups * quarter
    narrow = weights.shape[1] == half
    column = (lambda side: 0) if narrow else (lambda side: side[0])
    scale = 1.0 / math.sqrt(depth)
    block = lambda at: jnp.where(at < tiles, at, at - tiles)
    late = lambda at: jnp.maximum(at - tiles, 0)
    in_specs = [
        pl.BlockSpec((2 * tok, 1), lambda at, side: (0, 0)),
        pl.BlockSpec(
            (groups, None, quarter, feat),
            lambda at, side: (0, jnp.minimum(at, tiles - 1), 0, 0),
        ),
    ]
    operands = [ids, pieces, weights]
    if step == 0:
        in_specs.append(
            pl.BlockSpec((feat, half), lambda at, side: (jnp.minimum(at, tiles - 1), column(side)))
        )
        out_shape = jax.ShapeDtypeStruct((2, depth, half), jnp.bfloat16)
        out_spec = pl.BlockSpec((2, feat, half), lambda at, side: (0, late(at), 0))
    else:
        in_specs.append(pl.BlockSpec((feat, half), lambda at, side: (block(at), column(side))))
        in_specs.append(pl.BlockSpec((2, feat, half), lambda at, side: (0, block(at), 0)))
        operands.append(grad_one)
        out_shape = jax.ShapeDtypeStruct((depth, half), jnp.bfloat16)
        out_spec = pl.BlockSpec((feat, half), lambda at, side: (late(at), 0))
    in_specs += [
        pl.BlockSpec((None, tok, half), lambda at, side: (step, 0, column(side))),
        pl.BlockSpec((None, tok, half), lambda at, side: (step, 0, 0)),
    ]
    operands += [cot, cot_other]
    return pl.pallas_call(
        functools.partial(step_kernel, step, (tiles, tok, scale)),
        grid_spec=pltpu.PrefetchScalarGridSpec(
            num_scalar_prefetch=1,
            grid=(2 * tiles,),
            in_specs=in_specs,
            out_specs=out_spec,
            scratch_shapes=[
                pltpu.VMEM((2 * tok, rows), jnp.bfloat16),
                pltpu.VMEM((depth, 2 * tok), jnp.bfloat16),
                pltpu.VMEM((2 * tok, half), jnp.float32),
                pltpu.VMEM((2 * tok, half), jnp.bfloat16),
            ],
        ),
        out_shape=out_shape,
        compiler_params=pltpu.CompilerParams(vmem_limit_bytes=60 * 1024 * 1024),
        cost_estimate=pl.CostEstimate(
            flops=2 * 2 * tok * depth * (rows + 2 * half),
            bytes_accessed=60_000_000,
            transcendentals=0,
        ),
        name=f"inner_step_{step}",
    )(side, *operands)


def sum_update_kernel(islands, side, own, other, weights, momentum, held, fresh, placed):
    total = own[...].astype(jnp.float32) + other[...].astype(jnp.float32)
    mean = total * (1.0 / islands)
    moment = outer_moment * momentum[...].astype(jnp.float32) + mean
    base = weights[...].astype(jnp.float32)
    value = (base - outer_rate * (mean + outer_moment * moment)).astype(jnp.bfloat16)
    fresh[...] = value
    placed[...] = value


def plain_update(islands, chunk, own, other, weights, momentum):
    size = own.shape[0]
    span = slice(chunk * size, (chunk + 1) * size)
    mean = (own.astype(jnp.float32) + other.astype(jnp.float32)) / islands
    moment = outer_moment * momentum[span].astype(jnp.float32) + mean
    base = weights[span].astype(jnp.float32)
    return (base - outer_rate * (mean + outer_moment * moment)).astype(jnp.bfloat16)


def outer_update(islands, chunk, side, own, other, weights, momentum, held):
    size, half = own.shape
    rows = size // 2 if size % 32 == 0 else size
    steps = size // rows
    local = pl.BlockSpec((rows, half), lambda at, side: (at, 0))
    wide = pl.BlockSpec((rows, half), lambda at, side: (chunk * steps + at, side[0]))
    return pl.pallas_call(
        functools.partial(sum_update_kernel, islands),
        grid_spec=pltpu.PrefetchScalarGridSpec(
            num_scalar_prefetch=1,
            grid=(steps,),
            in_specs=[local, local, wide, wide, pl.BlockSpec(memory_space=pl.ANY)],
            out_specs=[local, wide],
        ),
        out_shape=[
            jax.ShapeDtypeStruct(own.shape, jnp.bfloat16),
            jax.ShapeDtypeStruct(held.shape, held.dtype),
        ],
        input_output_aliases={5: 1},
        compiler_params=pltpu.CompilerParams(vmem_limit_bytes=24 * 1024 * 1024),
        cost_estimate=pl.CostEstimate(
            flops=8 * size * half, bytes_accessed=12 * size * half, transcendentals=0
        ),
        name=f"outer_update_{chunk}",
    )(side, own, other, weights, momentum, held)


def place_kernel(side, block, held, placed):
    placed[...] = block[...]


def place(chunk, side, block, held):
    size, half = block.shape
    return pl.pallas_call(
        place_kernel,
        grid_spec=pltpu.PrefetchScalarGridSpec(
            num_scalar_prefetch=1,
            grid=(1,),
            in_specs=[
                pl.BlockSpec((size, half), lambda at, side: (0, 0)),
                pl.BlockSpec(memory_space=pl.ANY),
            ],
            out_specs=pl.BlockSpec((size, half), lambda at, side: (chunk, 1 - side[0])),
        ),
        out_shape=jax.ShapeDtypeStruct(held.shape, held.dtype),
        input_output_aliases={2: 0},
        compiler_params=pltpu.CompilerParams(vmem_limit_bytes=24 * 1024 * 1024),
        cost_estimate=pl.CostEstimate(
            flops=0, bytes_accessed=4 * size * half, transcendentals=0
        ),
        name=f"place_{chunk}",
    )(side, block, held)


def body(weights, momentum, table, token_ids, cotangent):
    islands = lax.axis_size("island")
    shards = lax.axis_size("fsdp")
    me = lax.axis_index("island")
    depth, columns = weights.shape
    half = columns // 2
    rows, feat = table.shape
    quarter = rows // islands
    partner = [(i, i ^ 1) for i in range(islands)]
    side = lax.rem(me, 2).astype(jnp.int32).reshape(1)

    mine = lax.dynamic_slice_in_dim(table, me * quarter, quarter, 0)
    pieces = lax.all_gather(mine, ("island", "fsdp"), axis=0, tiled=False)
    pieces = pieces.reshape(islands, shards, quarter, feat)

    cot = cotangent[0]
    ids_other = lax.ppermute(token_ids[0], "island", partner)
    to_send = lax.dynamic_slice_in_dim(cot, (1 - side[0]) * half, half, 2)
    cot_other = lax.ppermute(to_send, "island", partner)
    ids = jnp.stack([token_ids[0], ids_other], axis=1)

    steps, tok = token_ids.shape[1:]
    aligned = half % 128 == 0
    if not aligned:
        cot, weights, momentum = (take_half(a, side[0], half) for a in (cot, weights, momentum))
    grad_one = inner_step(
        0, side, ids[0].reshape(2 * tok, 1), pieces, weights, None, cot, cot_other
    )
    part = inner_step(
        1, side, ids[1].reshape(2 * tok, 1), pieces, weights, grad_one, cot, cot_other
    )

    held = jnp.zeros(weights.shape, jnp.bfloat16) if aligned else None
    size = depth // CHUNKS
    fresh, kept = [], []
    for chunk in range(CHUNKS):
        own = lax.slice_in_dim(part, chunk * size, (chunk + 1) * size, axis=0)
        reach = 2
        while reach < islands:
            other = lax.ppermute(own, "island", [(i, i ^ reach) for i in range(islands)])
            if 2 * reach < islands:
                own = (own.astype(jnp.float32) + other.astype(jnp.float32)).astype(jnp.bfloat16)
            reach *= 2
        if aligned:
            mine, held = outer_update(islands, chunk, side, own, other, weights, momentum, held)
        else:
            mine = plain_update(islands, chunk, own, other, weights, momentum)
            kept.append(mine)
        fresh.append(lax.ppermute(mine, "island", partner))
    if not aligned:
        low = jnp.concatenate(kept, axis=0)
        high = jnp.concatenate(fresh, axis=0)
        first = side[0] == 0
        return jnp.concatenate(
            [jnp.where(first, low, high), jnp.where(first, high, low)], axis=1
        )
    for chunk in range(CHUNKS):
        held = place(chunk, side, fresh[chunk], held)
    return held


def solution(mesh):
    placed = (
        P(None, "fsdp"),
        P(None, "fsdp"),
        P(None, "fsdp"),
        P("island", None, None),
        P("island", None, None, "fsdp"),
    )
    return jax.shard_map(
        body, mesh=mesh, in_specs=placed, out_specs=P(None, "fsdp"), check_vma=False
    )
```

time: 570 us -> 585 us (1.026)
  Pallas kernels: 0 us -> 204 us
  matrix products: 146 us -> 0 us
  waiting for transfers between devices: 377 us -> 313 us
  other arithmetic: 25.8 us -> 0.78 us
  starting transfers between devices: 0.09 us -> 23.1 us
  local copies, waits for them, and re-layouts: 8.6 us -> 30.1 us
    ppermute x0 -> x18, waiting for transfers between devices: none -> 275 us  [the longest x8 108 us: body(): lax.ppermute(own, 'island', [(i, i ^ reach) for i in range(islands)])]
    psum x1 -> x0, waiting for transfers between devices: 272 us -> none  [body(): total = lax.psum(delta.astype(jnp.bfloat16), 'island').astype(jnp.float32)]
    pallas_call x0 -> x18, Pallas kernels: none -> 204 us  [the longest x2 173 us: inner_step(): pl.pallas_call(functools.partial(step_kernel, step, (tiles, tok, scale)),...]
    dot_general x4 -> x0, matrix products: 146 us -> none  [the longest x2 84.7 us: grad_rows(): lax.dot_general(inputs, upstream, (((0,), (0,)), ((), ())), preferred_ele...]
    all_gather x2 -> x1, waiting for transfers between devices: 104 us -> 37.6 us  [body(): pieces = lax.all_gather(mine, ('island', 'fsdp'), axis=0, tiled=False)]
    convert_element_type x1 -> x0, other arithmetic: 23.5 us -> none  [outer_update(): (base - outer_rate * (mean + outer_moment * moment)).astype(jnp.bfloat16)]
    ppermute x0 -> x18, starting transfers between devices: none -> 23.1 us  [the longest x8 10.1 us: body(): lax.ppermute(own, 'island', [(i, i ^ reach) for i in range(islands)])]
    unnamed x6 -> x14, local copies, waits for them, and re-layouts: 0.7 us -> 11.1 us
  transfers between devices with their start and end apart: 3 -> 19, of which waited for: 3 -> 14; matrix products, arithmetic and copies ran while one was open for 8% -> 2% of each run, Pallas kernels for 0% -> 5%
where the time goes in v1:
time: 585 us; the launch traced here: 584 us
  waiting for transfers between devices  313 us (54%)
  Pallas kernels  204 us (35%)
  local copies, waits for them, and re-layouts  30.1 us (5%)
  starting transfers between devices  23.1 us (4%)
  between operations  13.4 us (2%)
    pallas_call x2, Pallas kernels, inner_step(): pl.pallas_call(functools.partial(step_kernel, step, (tiles, tok, scale)),...  173 us
    ppermute x8, waiting for transfers between devices, body(): lax.ppermute(own, 'island', [(i, i ^ reach) for i in range(islands)])  108 us
    ppermute x1, waiting for transfers between devices, body(): ids_other = lax.ppermute(token_ids[0], 'island', partner)  99.8 us
    ppermute x8, waiting for transfers between devices, body(): fresh.append(lax.ppermute(mine, 'island', partner))  67.1 us
    all_gather x1, waiting for transfers between devices, body(): pieces = lax.all_gather(mine, ('island', 'fsdp'), axis=0, tiled=False)  37.6 us
    pallas_call x8, Pallas kernels, outer_update(): pl.pallas_call(functools.partial(sum_update_kernel, islands), grid_spec=p...  22.6 us
  transfers between devices with their start and end apart: 19, of which 14 were waited for; matrix products, arithmetic and copies ran while one was open for 2% of the time, Pallas kernels for 5%

profile of v1, /device:TPU:0, one launch (start us, length us, event | category | flops | bytes accessed | tf_op | source)
XLA Modules:
  0.0 584.1 jit_solution(3893419422028799691)
XLA Ops:
  6.5 1.6 copy-done
  8.1 0.8 constant_dynamic-slice_fusion
  9.0 0.0 all-gather.3.cloned.1.call-update
  9.0 3.9 dynamic-slice_bitcast_fusion
  12.9 2.9 collective-permute-start.1
  15.8 0.0 collective-permute-start
  15.8 99.8 %collective-permute-done = s32[2,896]{1,0:T(2,128)S(1)} collective-permute-done((s32[2,896]{1,0:T(2,128)}, s32[2,896]{1,0:T(2,128)S(1)}, u32[]{:S(2)}, u32[]{:S(2)}) %collective-permute-start) | collective-permute-done | bytes 7200 | tf_op jit(solution)/shard_map/ppermute | solution.py:269
  115.6 0.8 pad_add_fusion
  116.4 1.3 copy.22.ids
  117.7 1.3 copy.23.ids
  118.9 37.6 %all-gather.3.cloned.1.call-done = bf16[16384,512]{1,0:T(8,128)(2,1)} async-done(((bf16[512,512]{1,0:T(8,128)(2,1)}), bf16[16384,512]{1,0:T(8,128)(2,1)}) %all-gather.3.cloned.1.call-update) | async-done | bytes 16777232 | tf_op jit(solution)/shard_map/all_gather | solution.py:265
  156.5 75.5 %inner_step_0.1.refs_0_ = bf16[2,4096,896]{2,1,0:T(8,128)(2,1)} custom-call(s32[1]{0:T(128)} %bitcast.side, s32[1792,1]{1,0:T(8,128)} %copy.22.ids, bf16[4,8,512,512]{3,2,1,0:T(8,128)(2,1)} %bitcast.17, bf16[4096,1792]{1,0:T(8,128)(2,1)} %weights.19, bf16[2,896,1792]{2,1,0:T(8,128)(2,1)} %bitcast.10, bf16[2,896,896]{2,1,0:T(8,128)(2,1)} %collective-permute-done.1.refs_1_.refs_2_), custom_call_target="tpu_custom_call" | custom-call | flops 56371445760 | bytes 60000000 | tf_op jit(solution)/shard_map/inner_step_0/pallas_call | solution.py:155
  232.0 97.9 %inner_step_1.1 = bf16[4096,896]{1,0:T(8,128)(2,1)} custom-call(s32[1]{0:T(128)} %bitcast.side, s32[1792,1]{1,0:T(8,128)} %copy.23.ids, bf16[4,8,512,512]{3,2,1,0:T(8,128)(2,1)} %bitcast.18, bf16[4096,1792]{1,0:T(8,128)(2,1)} %weights.19, bf16[2,4096,896]{2,1,0:T(8,128)(2,1)} %inner_step_0.1.refs_0_, bf16[2,896,1792]{2,1,0:T(8,128)(2,1)} %bitcast.11, ...), custom_call_target="tpu_custom_call" | custom-call | flops 56371445760 | bytes 60000000 | tf_op jit(solution)/shard_map/inner_step_1/pallas_call | solution.py:155
  330.0 5.4 fusion.1
  335.3 1.5 collective-permute-start.9
  336.8 1.0 copy-done.3
  337.9 0.5 collective-permute-start.8
  338.4 1.5 collective-permute-start.7
  339.9 0.5 collective-permute-start.6
  340.4 1.5 collective-permute-start.5
  341.9 16.6 %collective-permute-done.9.other = bf16[512,896]{1,0:T(8,128)(2,1)S(1)} collective-permute-done((bf16[512,896]{1,0:T(8,128)(2,1)S(1)}, bf16[512,896]{1,0:T(8,128)(2,1)S(1)}, u32[]{:S(2)}, u32[]{:S(2)}) %collective-permute-start.9) | collective-permute-done | bytes 917536 | tf_op jit(solution)/shard_map/ppermute | solution.py:292
  358.5 0.9 copy-done.5
  359.4 1.5 collective-permute-start.4
  360.9 6.4 %broadcast_in_dim.3.held = bf16[4096,1792]{1,0:T(8,128)(2,1)} broadcast(bf16[]{:T(256)} %constant.22.clone.1), dimensions={} | broadcast | bytes 14680066 | tf_op jit(solution)/shard_map/broadcast_in_dim | solution.py:285
  367.4 5.2 copy-done.2
  372.5 1.2 copy-done.4
  373.7 1.2 copy-done.6
  374.9 2.7 outer_update_0.1
  377.6 0.7 collective-permute-done.8.other
  378.3 1.5 collective-permute-start.3
  379.8 2.9 outer_update_1.1
  382.7 15.2 %collective-permute-done.7.other = bf16[512,896]{1,0:T(8,128)(2,1)} collective-permute-done((bf16[512,896]{1,0:T(8,128)(2,1)}, bf16[512,896]{1,0:T(8,128)(2,1)}, u32[]{:S(2)}, u32[]{:S(2)}) %collective-permute-start.7) | collective-permute-done | bytes 917536 | tf_op jit(solution)/shard_map/ppermute | solution.py:292
  397.9 1.5 collective-permute-start.2
  399.4 2.9 outer_update_2.1
  402.4 15.2 %collective-permute-done.6.other = bf16[512,896]{1,0:T(8,128)(2,1)} collective-permute-done((bf16[512,896]{1,0:T(8,128)(2,1)}, bf16[512,896]{1,0:T(8,128)(2,1)}, u32[]{:S(2)}, u32[]{:S(2)}) %collective-permute-start.6) | collective-permute-done | bytes 917536 | tf_op jit(solution)/shard_map/ppermute | solution.py:292
  417.6 1.5 collective-permute-start.17
  419.1 18.2 %collective-permute-done.5.other = bf16[512,896]{1,0:T(8,128)(2,1)} collective-permute-done((bf16[512,896]{1,0:T(8,128)(2,1)}, bf16[512,896]{1,0:T(8,128)(2,1)}, u32[]{:S(2)}, u32[]{:S(2)}) %collective-permute-start.5) | collective-permute-done | bytes 917536 | tf_op jit(solution)/shard_map/ppermute | solution.py:292
  437.2 1.5 collective-permute-start.16
  438.7 18.2 %collective-permute-done.4.other = bf16[512,896]{1,0:T(8,128)(2,1)} collective-permute-done((bf16[512,896]{1,0:T(8,128)(2,1)S(1)}, bf16[512,896]{1,0:T(8,128)(2,1)}, u32[]{:S(2)}, u32[]{:S(2)}) %collective-permute-start.4) | collective-permute-done | bytes 917536 | tf_op jit(solution)/shard_map/ppermute | solution.py:292
  456.9 1.5 collective-permute-start.15
  458.4 2.9 outer_update_3.1
  461.3 2.9 outer_update_4.1
  464.3 2.8 outer_update_5.1
  467.1 9.4 %collective-permute-done.3.other = bf16[512,896]{1,0:T(8,128)(2,1)S(1)} collective-permute-done((bf16[512,896]{1,0:T(8,128)(2,1)S(1)}, bf16[512,896]{1,0:T(8,128)(2,1)S(1)}, u32[]{:S(2)}, u32[]{:S(2)}) %collective-permute-start.3) | collective-permute-done | bytes 917536 | tf_op jit(solution)/shard_map/ppermute | solution.py:292
  476.5 1.5 collective-permute-start.14
  478.0 2.7 outer_update_6.1
  480.6 14.8 %collective-permute-done.2.other = bf16[512,896]{1,0:T(8,128)(2,1)S(1)} collective-permute-done((bf16[512,896]{1,0:T(8,128)(2,1)S(1)}, bf16[512,896]{1,0:T(8,128)(2,1)S(1)}, u32[]{:S(2)}, u32[]{:S(2)}) %collective-permute-start.2) | collective-permute-done | bytes 917536 | tf_op jit(solution)/shard_map/ppermute | solution.py:292
  495.5 1.5 collective-permute-start.13
  497.0 2.7 outer_update_7.1
  499.6 0.6 collective-permute-start.12
  500.2 1.5 collective-permute-start.11
  501.7 0.6 collective-permute-start.10
  502.2 1.0 place_0.1.held
  503.2 1.0 place_1.1.held
  504.2 1.0 place_2.1.held
  505.2 1.0 place_3.1.held
  506.2 12.5 %collective-permute-done.13.block = bf16[512,896]{1,0:T(8,128)(2,1)S(1)} collective-permute-done((bf16[512,896]{1,0:T(8,128)(2,1)S(1)}, bf16[512,896]{1,0:T(8,128)(2,1)S(1)}, u32[]{:S(2)}, u32[]{:S(2)}) %collective-permute-start.13) | collective-permute-done | bytes 917536 | tf_op jit(solution)/shard_map/ppermute | solution.py:301
  518.8 1.0 place_4.1.held
  519.7 18.7 %collective-permute-done.12.block = bf16[512,896]{1,0:T(8,128)(2,1)S(1)} collective-permute-done((bf16[512,896]{1,0:T(8,128)(2,1)S(1)}, bf16[512,896]{1,0:T(8,128)(2,1)S(1)}, u32[]{:S(2)}, u32[]{:S(2)}) %collective-permute-start.12) | collective-permute-done | bytes 917536 | tf_op jit(solution)/shard_map/ppermute | solution.py:301
  538.4 1.0 place_5.1.held
  539.4 18.7 %collective-permute-done.11.block = bf16[512,896]{1,0:T(8,128)(2,1)S(1)} collective-permute-done((bf16[512,896]{1,0:T(8,128)(2,1)S(1)}, bf16[512,896]{1,0:T(8,128)(2,1)S(1)}, u32[]{:S(2)}, u32[]{:S(2)}) %collective-permute-start.11) | collective-permute-done | bytes 917536 | tf_op jit(solution)/shard_map/ppermute | solution.py:301
  558.1 1.0 place_6.1.held
  559.1 17.2 %collective-permute-done.10.block = bf16[512,896]{1,0:T(8,128)(2,1)S(1)} collective-permute-done((bf16[512,896]{1,0:T(8,128)(2,1)S(1)}, bf16[512,896]{1,0:T(8,128)(2,1)S(1)}, u32[]{:S(2)}, u32[]{:S(2)}) %collective-permute-start.10) | collective-permute-done | bytes 917536 | tf_op jit(solution)/shard_map/ppermute | solution.py:301
  576.3 1.0 place_7.1
  (14 shorter events, 0.0 us)
Async XLA Ops:
  6.5 1.6 copy-start
  6.5 150.0 %all-gather.3.cloned.1.call-start = ((), (), s32[]{:S(2)}) async-start(), calls=%async_computation | async-start | bytes 17301504 | tf_op jit(solution)/shard_map/all_gather | solution.py:265
  12.9 106.1 %collective-permute-start.1 = (bf16[2,896,896]{2,1,0:T(8,128)(2,1)}, bf16[2,896,896]{2,1,0:T(8,128)(2,1)}, u32[]{:S(2)}, u32[]{:S(2)}) collective-permute-start(bf16[2,896,896]{2,1,0:T(8,128)(2,1)} %dynamic-slice_bitcast_fusion), channel_id=1, source_target_pairs={{0,8},{8,0},{16,24},{24,16},{1,9},{9,1},{17,25},{25,17},{2,10},{10... | collective-permute-start | bytes 9633800 | tf_op jit(solution)/shard_map/ppermute | solution.py:271
  15.8 99.8 %collective-permute-start = (s32[2,896]{1,0:T(2,128)}, s32[2,896]{1,0:T(2,128)S(1)}, u32[]{:S(2)}, u32[]{:S(2)}) collective-permute-start(s32[2,896]{1,0:T(2,128)} %bitcast.14), channel_id=1, source_target_pairs={{0,8},{8,0},{16,24},{24,16},{1,9},{9,1},{17,25},{25,17},{2,10},{10... | collective-permute-start | bytes 21512 | tf_op jit(solution)/shard_map/ppermute | solution.py:269
  335.3 23.2 %collective-permute-start.9 = (bf16[512,896]{1,0:T(8,128)(2,1)S(1)}, bf16[512,896]{1,0:T(8,128)(2,1)S(1)}, u32[]{:S(2)}, u32[]{:S(2)}) collective-permute-start(bf16[512,896]{1,0:T(8,128)(2,1)S(1)} %get-tuple-element.37.own), channel_id=1, source_target_pairs={{0,16},{8,24},{16,0},{24,8},{1,17},{9,25},{17,1},{25,9},{2,18},{10... | collective-permute-start | bytes 2752520 | tf_op jit(solution)/shard_map/ppermute | solution.py:292
  336.8 1.0 copy-start.3
  337.9 40.4 %collective-permute-start.8 = (bf16[512,896]{1,0:T(8,128)(2,1)}, bf16[512,896]{1,0:T(8,128)(2,1)}, u32[]{:S(2)}, u32[]{:S(2)}) collective-permute-start(bf16[512,896]{1,0:T(8,128)(2,1)} %get-tuple-element.38.own), channel_id=1, source_target_pairs={{0,16},{8,24},{16,0},{24,8},{1,17},{9,25},{17,1},{25,9},{2,18},{10... | collective-permute-start | bytes 2752520 | tf_op jit(solution)/shard_map/ppermute | solution.py:292
  338.4 59.6 %collective-permute-start.7 = (bf16[512,896]{1,0:T(8,128)(2,1)}, bf16[512,896]{1,0:T(8,128)(2,1)}, u32[]{:S(2)}, u32[]{:S(2)}) collective-permute-start(bf16[512,896]{1,0:T(8,128)(2,1)} %get-tuple-element.39.own), channel_id=1, source_target_pairs={{0,16},{8,24},{16,0},{24,8},{1,17},{9,25},{17,1},{25,9},{2,18},{10... | collective-permute-start | bytes 2752520 | tf_op jit(solution)/shard_map/ppermute | solution.py:292
  339.9 77.7 %collective-permute-start.6 = (bf16[512,896]{1,0:T(8,128)(2,1)}, bf16[512,896]{1,0:T(8,128)(2,1)}, u32[]{:S(2)}, u32[]{:S(2)}) collective-permute-start(bf16[512,896]{1,0:T(8,128)(2,1)} %get-tuple-element.40.own), channel_id=1, source_target_pairs={{0,16},{8,24},{16,0},{24,8},{1,17},{9,25},{17,1},{25,9},{2,18},{10... | collective-permute-start | bytes 2752520 | tf_op jit(solution)/shard_map/ppermute | solution.py:292
  340.4 96.9 %collective-permute-start.5 = (bf16[512,896]{1,0:T(8,128)(2,1)}, bf16[512,896]{1,0:T(8,128)(2,1)}, u32[]{:S(2)}, u32[]{:S(2)}) collective-permute-start(bf16[512,896]{1,0:T(8,128)(2,1)} %get-tuple-element.41.own), channel_id=1, source_target_pairs={{0,16},{8,24},{16,0},{24,8},{1,17},{9,25},{17,1},{25,9},{2,18},{10... | collective-permute-start | bytes 2752520 | tf_op jit(solution)/shard_map/ppermute | solution.py:292
  358.5 0.9 copy-start.5
  359.4 97.5 %collective-permute-start.4 = (bf16[512,896]{1,0:T(8,128)(2,1)S(1)}, bf16[512,896]{1,0:T(8,128)(2,1)}, u32[]{:S(2)}, u32[]{:S(2)}) collective-permute-start(bf16[512,896]{1,0:T(8,128)(2,1)S(1)} %get-tuple-element.42.own), channel_id=1, source_target_pairs={{0,16},{8,24},{16,0},{24,8},{1,17},{9,25},{17,1},{25,9},{2,18},{10... | collective-permute-start | bytes 2752520 | tf_op jit(solution)/shard_map/ppermute | solution.py:292
  367.3 5.2 copy-start.2
  372.5 1.2 copy-start.4
  373.7 1.2 copy-start.6
  378.3 98.2 %collective-permute-start.3 = (bf16[512,896]{1,0:T(8,128)(2,1)S(1)}, bf16[512,896]{1,0:T(8,128)(2,1)S(1)}, u32[]{:S(2)}, u32[]{:S(2)}) collective-permute-start(bf16[512,896]{1,0:T(8,128)(2,1)S(1)} %get-tuple-element.43.own), channel_id=1, source_target_pairs={{0,16},{8,24},{16,0},{24,8},{1,17},{9,25},{17,1},{25,9},{2,18},{10... | collective-permute-start | bytes 2752520 | tf_op jit(solution)/shard_map/ppermute | solution.py:292
  397.9 97.5 %collective-permute-start.2 = (bf16[512,896]{1,0:T(8,128)(2,1)S(1)}, bf16[512,896]{1,0:T(8,128)(2,1)S(1)}, u32[]{:S(2)}, u32[]{:S(2)}) collective-permute-start(bf16[512,896]{1,0:T(8,128)(2,1)S(1)} %get-tuple-element.44.own), channel_id=1, source_target_pairs={{0,16},{8,24},{16,0},{24,8},{1,17},{9,25},{17,1},{25,9},{2,18},{10... | collective-permute-start | bytes 2752520 | tf_op jit(solution)/shard_map/ppermute | solution.py:292
  417.6 82.1 %collective-permute-start.17 = (bf16[512,896]{1,0:T(8,128)(2,1)S(1)}, bf16[512,896]{1,0:T(8,128)(2,1)S(1)}, u32[]{:S(2)}, u32[]{:S(2)}) collective-permute-start(bf16[512,896]{1,0:T(8,128)(2,1)S(1)} %get-tuple-element.35), channel_id=1, source_target_pairs={{0,8},{8,0},{16,24},{24,16},{1,9},{9,1},{17,25},{25,17},{2,10},{10... | collective-permute-start | bytes 2752520 | tf_op jit(solution)/shard_map/ppermute | solution.py:301
  437.2 63.0 %collective-permute-start.16 = (bf16[512,896]{1,0:T(8,128)(2,1)S(1)}, bf16[512,896]{1,0:T(8,128)(2,1)S(1)}, u32[]{:S(2)}, u32[]{:S(2)}) collective-permute-start(bf16[512,896]{1,0:T(8,128)(2,1)S(1)} %get-tuple-element.34), channel_id=1, source_target_pairs={{0,8},{8,0},{16,24},{24,16},{1,9},{9,1},{17,25},{25,17},{2,10},{10... | collective-permute-start | bytes 2752520 | tf_op jit(solution)/shard_map/ppermute | solution.py:301
  456.9 44.8 %collective-permute-start.15 = (bf16[512,896]{1,0:T(8,128)(2,1)S(1)}, bf16[512,896]{1,0:T(8,128)(2,1)S(1)}, u32[]{:S(2)}, u32[]{:S(2)}) collective-permute-start(bf16[512,896]{1,0:T(8,128)(2,1)S(1)} %get-tuple-element.33), channel_id=1, source_target_pairs={{0,8},{8,0},{16,24},{24,16},{1,9},{9,1},{17,25},{25,17},{2,10},{10... | collective-permute-start | bytes 2752520 | tf_op jit(solution)/shard_map/ppermute | solution.py:301
  476.5 28.7 %collective-permute-start.14 = (bf16[512,896]{1,0:T(8,128)(2,1)S(1)}, bf16[512,896]{1,0:T(8,128)(2,1)S(1)}, u32[]{:S(2)}, u32[]{:S(2)}) collective-permute-start(bf16[512,896]{1,0:T(8,128)(2,1)S(1)} %get-tuple-element.32), channel_id=1, source_target_pairs={{0,8},{8,0},{16,24},{24,16},{1,9},{9,1},{17,25},{25,17},{2,10},{10... | collective-permute-start | bytes 2752520 | tf_op jit(solution)/shard_map/ppermute | solution.py:301
  495.5 23.3 %collective-permute-start.13 = (bf16[512,896]{1,0:T(8,128)(2,1)S(1)}, bf16[512,896]{1,0:T(8,128)(2,1)S(1)}, u32[]{:S(2)}, u32[]{:S(2)}) collective-permute-start(bf16[512,896]{1,0:T(8,128)(2,1)S(1)} %get-tuple-element.31), channel_id=1, source_target_pairs={{0,8},{8,0},{16,24},{24,16},{1,9},{9,1},{17,25},{25,17},{2,10},{10... | collective-permute-start | bytes 2752520 | tf_op jit(solution)/shard_map/ppermute | solution.py:301
  499.6 38.8 %collective-permute-start.12 = (bf16[512,896]{1,0:T(8,128)(2,1)S(1)}, bf16[512,896]{1,0:T(8,128)(2,1)S(1)}, u32[]{:S(2)}, u32[]{:S(2)}) collective-permute-start(bf16[512,896]{1,0:T(8,128)(2,1)S(1)} %get-tuple-element.30), channel_id=1, source_target_pairs={{0,8},{8,0},{16,24},{24,16},{1,9},{9,1},{17,25},{25,17},{2,10},{10... | collective-permute-start | bytes 2752520 | tf_op jit(solution)/shard_map/ppermute | solution.py:301
  500.2 57.9 %collective-permute-start.11 = (bf16[512,896]{1,0:T(8,128)(2,1)S(1)}, bf16[512,896]{1,0:T(8,128)(2,1)S(1)}, u32[]{:S(2)}, u32[]{:S(2)}) collective-permute-start(bf16[512,896]{1,0:T(8,128)(2,1)S(1)} %get-tuple-element.29), channel_id=1, source_target_pairs={{0,8},{8,0},{16,24},{24,16},{1,9},{9,1},{17,25},{25,17},{2,10},{10... | collective-permute-start | bytes 2752520 | tf_op jit(solution)/shard_map/ppermute | solution.py:301
  501.7 74.6 %collective-permute-start.10 = (bf16[512,896]{1,0:T(8,128)(2,1)S(1)}, bf16[512,896]{1,0:T(8,128)(2,1)S(1)}, u32[]{:S(2)}, u32[]{:S(2)}) collective-permute-start(bf16[512,896]{1,0:T(8,128)(2,1)S(1)} %get-tuple-element.28), channel_id=1, source_target_pairs={{0,8},{8,0},{16,24},{24,16},{1,9},{9,1},{17,25},{25,17},{2,10},{10... | collective-permute-start | bytes 2752520 | tf_op jit(solution)/shard_map/ppermute | solution.py:301
  558.1 19.2 %copy-start.1 = (bf16[2048,512]{1,0:T(8,128)(2,1)S(1)}, bf16[2048,512]{1,0:T(8,128)(2,1)}, u32[]{:S(2)}) copy-start(bf16[2048,512]{1,0:T(8,128)(2,1)} %param.7) | copy-start | bytes 6291460
Sparse Core Ops, SparseCore 0:
  10.4 146.0 all-gather.2

commit v2 on v1

v2 whole, which is shorter than its diff:
```python
import functools
import math

import jax
import jax.numpy as jnp
from jax import lax
from jax.experimental import pallas as pl
from jax.experimental.pallas import tpu as pltpu
from jax.sharding import PartitionSpec as P

beta_one = 0.9
beta_two = 0.95
adam_eps = 0.0001
inner_rate = 0.1
decay_rate = 0.1
outer_rate = 0.7
outer_moment = 0.9

CHUNKS = 8


def silu_slope(hidden):
    sigma = jax.nn.sigmoid(hidden)
    return sigma * (1.0 + hidden * (1.0 - sigma))


def first_move(grad):
    return grad / (jnp.abs(grad) + adam_eps)


def second_move(grad_one, grad_two):
    first = beta_one * (1.0 - beta_one) * grad_one + (1.0 - beta_one) * grad_two
    second = (
        beta_two * (1.0 - beta_two) * grad_one * grad_one
        + (1.0 - beta_two) * grad_two * grad_two
    )
    m_hat = first * (1.0 / (1.0 - beta_one**2))
    v_hat = second * (1.0 / (1.0 - beta_two**2))
    return m_hat / (jnp.sqrt(v_hat) + adam_eps)


def params(mib):
    return pltpu.CompilerParams(vmem_limit_bytes=mib * 1024 * 1024)


def pick_kernel(part, tok, side, ids, pieces, weights, *refs):
    early, late, hidden, picks = refs[-4:]
    rows, feat = picks.shape[1], pieces.shape[-1]

    @pl.when(pl.program_id(0) == 0)
    def _():
        hidden[...] = jnp.zeros_like(hidden) if part == 0 else refs[0][...]

        @pl.loop(0, 4 * tok // 128)
        def _(block):
            span = pl.ds(pl.multiple_of(block * 128, 128), 128)
            row = lax.broadcasted_iota(jnp.int32, (128, rows), 1)
            picks[span, :] = (row == ids[span, :]).astype(jnp.float32).astype(jnp.bfloat16)

    shard = pieces[...].reshape(rows, feat)
    for island in range(2):
        span = pl.ds(island * tok, tok)
        chosen = jnp.dot(picks[span, :], shard, preferred_element_type=jnp.float32)
        chosen = chosen.astype(jnp.bfloat16)
        early[island] = chosen.T
        hidden[span, :] += jnp.dot(chosen, weights[...], preferred_element_type=jnp.float32)
        chosen = jnp.dot(
            picks[pl.ds((2 + island) * tok, tok), :], shard, preferred_element_type=jnp.float32
        )
        late[island] = chosen.astype(jnp.bfloat16).T


def pick(part, parts, column, side, ids, pieces, weights, half, behind):
    groups, tiles, quarter, feat = pieces.shape
    tok = ids.shape[0] // 4
    whole = pl.BlockSpec((2 * tok, half), lambda at, side: (0, 0), pipeline_mode=pl.Buffered(1))
    in_specs = [
        pl.BlockSpec((4 * tok, 1), lambda at, side: (0, 0), pipeline_mode=pl.Buffered(1)),
        pl.BlockSpec((groups, None, quarter, feat), lambda at, side: (0, at, 0, 0)),
        pl.BlockSpec((feat, half), lambda at, side: (parts * at + part, column(side))),
    ]
    operands = [ids, pieces, weights]
    if part:
        in_specs += [whole] + [pl.BlockSpec(memory_space=pl.ANY)] * 2
        operands += behind
    return pl.pallas_call(
        functools.partial(pick_kernel, part, tok),
        grid_spec=pltpu.PrefetchScalarGridSpec(
            num_scalar_prefetch=1,
            grid=(tiles,),
            in_specs=in_specs,
            out_specs=[
                pl.BlockSpec((2, None, feat, tok), lambda at, side: (0, part, at, 0)),
                pl.BlockSpec((2, None, feat, tok), lambda at, side: (0, part, at, 0)),
                pl.BlockSpec((2 * tok, half), lambda at, side: (0, 0)),
            ],
            scratch_shapes=[pltpu.VMEM((4 * tok, groups * quarter), jnp.bfloat16)],
        ),
        out_shape=[
            jax.ShapeDtypeStruct((2, parts, tiles * feat, tok), jnp.bfloat16),
            jax.ShapeDtypeStruct((2, parts, tiles * feat, tok), jnp.bfloat16),
            jax.ShapeDtypeStruct((2 * tok, half), jnp.float32),
        ],
        input_output_aliases={4: 2, 5: 0, 6: 1} if part else {},
        compiler_params=params(56),
        cost_estimate=pl.CostEstimate(
            flops=2 * 2 * tok * tiles * feat * (2 * groups * quarter + half),
            bytes_accessed=50_000_000,
            transcendentals=0,
        ),
        name=f"pick_{part}",
    )(side, *operands)


def make_upstream(hidden, cots, scale, upstream):
    tok = cots[0].shape[0]
    for island, cot in enumerate(cots):

        @pl.loop(0, tok // 128)
        def _(part):
            inner = pl.ds(pl.multiple_of(part * 128, 128), 128)
            span = pl.ds(pl.multiple_of(island * tok + part * 128, 128), 128)
            value = cot[inner, :].astype(jnp.float32) * silu_slope(hidden[span, :] * scale)
            upstream[span, :] = (value * (1.0 / tok)).astype(jnp.bfloat16)


def middle_kernel(
    scale, side, hidden, own, other, own_late, other_late, early, late, weights,
    grad_one, upstream_late, upstream, hidden_late,
):
    tok = own.shape[0]
    parts, part = early.shape[1:3]
    keep = 1.0 - inner_rate * decay_rate
    at = pl.program_id(0)

    @pl.when(at == 0)
    def _():
        make_upstream(hidden, (own, other), scale, upstream)
        hidden_late[...] = jnp.zeros_like(hidden_late)

    @pl.loop(0, parts)
    def _(index):
        place = pl.ds(pl.multiple_of(index * part, part), part)
        base = weights[place, :].astype(jnp.float32)
        for island in range(2):
            span = pl.ds(island * tok, tok)
            grad = scale * jnp.dot(
                early[island, index], upstream[span, :], preferred_element_type=jnp.float32
            )
            grad_one[island, index] = grad.astype(jnp.bfloat16)
            work = (keep * base - inner_rate * first_move(grad)).astype(jnp.bfloat16)
            hidden_late[span, :] += jnp.dot(
                late[island, index].T, work, preferred_element_type=jnp.float32
            )

    @pl.when(at == pl.num_programs(0) - 1)
    def _():
        make_upstream(hidden_late, (own_late, other_late), scale, upstream_late)


def middle(tiles, column, side, hidden, cot, cot_other, early, late, weights):
    double, half = hidden.shape
    tok = double // 2
    depth = weights.shape[0]
    parts = early.shape[1]
    part = early.shape[2] // tiles
    once = pl.Buffered(1)
    cot_spec = lambda step, side_of: pl.BlockSpec(
        (None, tok, half), lambda at, side: (step, 0, side_of(side)), pipeline_mode=once
    )
    none = lambda side: 0
    tall = lambda width: pl.BlockSpec((2, parts, part, width), lambda at, side: (0, 0, at, 0))
    return pl.pallas_call(
        functools.partial(middle_kernel, 1.0 / math.sqrt(depth)),
        grid_spec=pltpu.PrefetchScalarGridSpec(
            num_scalar_prefetch=1,
            grid=(tiles,),
            in_specs=[
                pl.BlockSpec((double, half), lambda at, side: (0, 0), pipeline_mode=once),
                cot_spec(0, column),
                cot_spec(0, none),
                cot_spec(1, column),
                cot_spec(1, none),
                tall(tok),
                tall(tok),
                pl.BlockSpec((parts * part, half), lambda at, side: (at, column(side))),
            ],
            out_specs=[
                tall(half),
                pl.BlockSpec((double, half), lambda at, side: (0, 0)),
            ],
            scratch_shapes=[
                pltpu.VMEM((double, half), jnp.bfloat16),
                pltpu.VMEM((double, half), jnp.float32),
            ],
        ),
        out_shape=[
            jax.ShapeDtypeStruct(early.shape[:3] + (half,), jnp.bfloat16),
            jax.ShapeDtypeStruct((double, half), jnp.bfloat16),
        ],
        input_output_aliases={6: 0} if tok == half else {},
        compiler_params=params(60),
        cost_estimate=pl.CostEstimate(
            flops=2 * 2 * double * depth * half, bytes_accessed=90_000_000, transcendentals=0
        ),
        name="middle",
    )(side, hidden, cot, cot_other, cot, cot_other, early, late, weights)


def last_kernel(scale, side, late, upstream, grad_one, weights, *refs):
    out = refs[-1]
    tok = upstream.shape[0] // 2
    parts, part = late.shape[1:3]
    keep = 1.0 - inner_rate * decay_rate

    @pl.loop(0, parts * part // 128)
    def _(block):
        index, row = block // (part // 128), block % (part // 128)
        place = pl.ds(pl.multiple_of(block * 128, 128), 128)
        rows = pl.ds(pl.multiple_of(row * 128, 128), 128)
        total = (2.0 * (1.0 - keep * keep)) * weights[place, :].astype(jnp.float32)
        for island in range(2):
            span = pl.ds(island * tok, tok)
            grad = scale * jnp.dot(
                late[island, index, rows, :], upstream[span, :], preferred_element_type=jnp.float32
            )
            one = grad_one[island, index, rows, :].astype(jnp.float32)
            total += (keep * inner_rate) * first_move(one)
            total += inner_rate * second_move(one, grad)
        out[place, :] = total.astype(jnp.bfloat16)


def last(chunk, tiles, column, side, late, upstream, grad_one, weights, after):
    double, half = upstream.shape
    depth = weights.shape[0]
    size = depth // CHUNKS
    rows = depth // tiles
    steps = size // rows
    parts, tok = late.shape[1], late.shape[3]
    block = (2, parts, rows // parts)
    row = lambda at: chunk * steps + at
    return pl.pallas_call(
        functools.partial(last_kernel, 1.0 / math.sqrt(depth)),
        grid_spec=pltpu.PrefetchScalarGridSpec(
            num_scalar_prefetch=1,
            grid=(steps,),
            in_specs=[
                pl.BlockSpec(block + (tok,), lambda at, side: (0, 0, row(at), 0)),
                pl.BlockSpec((double, half), lambda at, side: (0, 0)),
                pl.BlockSpec(block + (half,), lambda at, side: (0, 0, row(at), 0)),
                pl.BlockSpec((rows, half), lambda at, side: (row(at), column(side))),
            ]
            + [pl.BlockSpec(memory_space=pl.ANY)] * len(after),
            out_specs=pl.BlockSpec((rows, half), lambda at, side: (at, 0)),
        ),
        out_shape=jax.ShapeDtypeStruct((size, half), jnp.bfloat16),
        compiler_params=params(60),
        cost_estimate=pl.CostEstimate(
            flops=2 * double * size * half, bytes_accessed=10_000_000, transcendentals=0
        ),
        name=f"last_{chunk}",
    )(side, late, upstream, grad_one, weights, *after)


def take_half(array, which, half):
    return lax.dynamic_slice_in_dim(array, which * half, half, array.ndim - 1)


def plain_update(islands, chunk, own, other, weights, momentum):
    size = own.shape[0]
    span = slice(chunk * size, (chunk + 1) * size)
    mean = (own.astype(jnp.float32) + other.astype(jnp.float32)) / islands
    moment = outer_moment * momentum[span].astype(jnp.float32) + mean
    base = weights[span].astype(jnp.float32)
    return (base - outer_rate * (mean + outer_moment * moment)).astype(jnp.bfloat16)


def sum_update_kernel(islands, side, own, other, weights, momentum, *refs):
    fresh, placed = refs[-2:]
    total = own[...].astype(jnp.float32) + other[...].astype(jnp.float32)
    mean = total * (1.0 / islands)
    moment = outer_moment * momentum[...].astype(jnp.float32) + mean
    base = weights[...].astype(jnp.float32)
    value = (base - outer_rate * (mean + outer_moment * moment)).astype(jnp.bfloat16)
    fresh[...] = value
    placed[...] = value


def outer_update(islands, chunk, side, own, other, weights, momentum, held):
    size, half = own.shape
    rows = size // 2 if size % 32 == 0 else size
    steps = size // rows
    behind = [] if held is None else [held]
    local = pl.BlockSpec((rows, half), lambda at, side: (at, 0))
    wide = pl.BlockSpec((rows, half), lambda at, side: (chunk * steps + at, side[0]))
    return pl.pallas_call(
        functools.partial(sum_update_kernel, islands),
        grid_spec=pltpu.PrefetchScalarGridSpec(
            num_scalar_prefetch=1,
            grid=(steps,),
            in_specs=[local, local, wide, wide]
            + [pl.BlockSpec(memory_space=pl.ANY)] * len(behind),
            out_specs=[local, wide],
        ),
        out_shape=[
            jax.ShapeDtypeStruct(own.shape, jnp.bfloat16),
            jax.ShapeDtypeStruct(weights.shape, weights.dtype),
        ],
        input_output_aliases={5: 1} if behind else {},
        compiler_params=params(60),
        cost_estimate=pl.CostEstimate(
            flops=8 * size * half, bytes_accessed=12 * size * half, transcendentals=0
        ),
        name=f"outer_update_{chunk}",
    )(side, own, other, weights, momentum, *behind)


def place_kernel(side, block, held, placed):
    placed[...] = block[...]


def place(chunk, side, block, held):
    size, half = block.shape
    return pl.pallas_call(
        place_kernel,
        grid_spec=pltpu.PrefetchScalarGridSpec(
            num_scalar_prefetch=1,
            grid=(1,),
            in_specs=[
                pl.BlockSpec((size, half), lambda at, side: (0, 0)),
                pl.BlockSpec(memory_space=pl.ANY),
            ],
            out_specs=pl.BlockSpec((size, half), lambda at, side: (chunk, 1 - side[0])),
        ),
        out_shape=jax.ShapeDtypeStruct(held.shape, held.dtype),
        input_output_aliases={2: 0},
        compiler_params=params(60),
        cost_estimate=pl.CostEstimate(
            flops=0, bytes_accessed=4 * size * half, transcendentals=0
        ),
        name=f"place_{chunk}",
    )(side, block, held)


def body(weights, momentum, table, token_ids, cotangent):
    islands = lax.axis_size("island")
    shards = lax.axis_size("fsdp")
    me = lax.axis_index("island")
    depth, columns = weights.shape
    half = columns // 2
    rows, feat = table.shape
    quarter = rows // islands
    partner = [(i, i ^ 1) for i in range(islands)]
    side = lax.rem(me, 2).astype(jnp.int32).reshape(1)

    parts = 2
    mine = lax.dynamic_slice_in_dim(table, me * quarter, quarter, 0)
    pieces = []
    for part in range(parts):
        cut = lax.slice_in_dim(mine, part * feat // parts, (part + 1) * feat // parts, axis=1)
        got = lax.all_gather(cut, ("island", "fsdp"), axis=0, tiled=False)
        pieces.append(got.reshape(islands, shards, quarter, feat // parts))

    cot = cotangent[0]
    ids_other = lax.ppermute(token_ids[0], "island", partner)
    to_send = lax.dynamic_slice_in_dim(cot, (1 - side[0]) * half, half, 2)
    cot_other = lax.ppermute(to_send, "island", partner)
    ids = jnp.stack([token_ids[0], ids_other], axis=1)

    steps, tok = token_ids.shape[1:]
    aligned = half % 128 == 0
    if not aligned:
        cot, weights, momentum = (take_half(a, side[0], half) for a in (cot, weights, momentum))
    column = (lambda side: side[0]) if aligned else (lambda side: 0)
    ids = ids.reshape(2 * steps * tok, 1)
    behind = []
    for part in range(parts):
        early, late, hidden = pick(
            part, parts, column, side, ids, pieces[part], weights, half, behind
        )
        behind = [hidden, early, late]
    grad_one, upstream = middle(
        shards, column, side, hidden, cot, cot_other, early, late, weights
    )

    held = None
    size = depth // CHUNKS
    fresh, kept, arrived = [], [], []
    for chunk in range(CHUNKS):
        after = [a[chunk - n] for a, n in ((arrived, 2), (fresh, 3)) if chunk >= n]
        own = last(chunk, shards, column, side, late, upstream, grad_one, weights, after)
        reach = 2
        while reach < islands:
            other = lax.ppermute(own, "island", [(i, i ^ reach) for i in range(islands)])
            if 2 * reach < islands:
                own = (own.astype(jnp.float32) + other.astype(jnp.float32)).astype(jnp.bfloat16)
            reach *= 2
        arrived.append(other)
        if aligned:
            mine, held = outer_update(islands, chunk, side, own, other, weights, momentum, held)
        else:
            mine = plain_update(islands, chunk, own, other, weights, momentum)
            kept.append(mine)
        fresh.append(lax.ppermute(mine, "island", partner))
    if not aligned:
        low = jnp.concatenate(kept, axis=0)
        high = jnp.concatenate(fresh, axis=0)
        first = side[0] == 0
        return jnp.concatenate(
            [jnp.where(first, low, high), jnp.where(first, high, low)], axis=1
        )
    for chunk in range(CHUNKS):
        held = place(chunk, side, fresh[chunk], held)
    return held


def solution(mesh):
    placed = (
        P(None, "fsdp"),
        P(None, "fsdp"),
        P(None, "fsdp"),
        P("island", None, None),
        P("island", None, None, "fsdp"),
    )
    return jax.shard_map(
        body, mesh=mesh, in_specs=placed, out_specs=P(None, "fsdp"), check_vma=False
    )
```

time: 585 us -> 522 us (0.89)
  waiting for transfers between devices: 313 us -> 184 us
  Pallas kernels: 204 us -> 279 us
  local copies, waits for them, and re-layouts: 30.1 us -> 20.3 us
    ppermute x1, waiting for transfers between devices: 99.8 us -> 0.01 us  [body(): ids_other = lax.ppermute(token_ids[0], 'island', partner)]
    all_gather x1 -> x2, waiting for transfers between devices: 37.6 us -> 125 us  [body(): got = lax.all_gather(cut, ('island', 'fsdp'), axis=0, tiled=False)]
    ppermute x8, waiting for transfers between devices: 108 us -> 32.2 us  [body(): lax.ppermute(own, 'island', [(i, i ^ reach) for i in range(islands)])]
    pallas_call x2 -> x11, Pallas kernels: 173 us -> 235 us  [the longest x2 103 us: pick(): pl.pallas_call(functools.partial(pick_kernel, part, tok), grid_spec=pltpu...]
    ppermute x8, waiting for transfers between devices: 67.1 us -> 26 us  [body(): fresh.append(lax.ppermute(mine, 'island', partner))]
    pallas_call x8, Pallas kernels: 7.92 us -> 17.3 us  [place(): pl.pallas_call(place_kernel, grid_spec=pltpu.PrefetchScalarGridSpec(num_s...]
    broadcast_in_dim x1 -> x0, local copies, waits for them, and re-layouts: 6.41 us -> none  [body(): held = jnp.zeros(weights.shape, jnp.bfloat16) if aligned else None]
    unnamed x14 -> x30, local copies, waits for them, and re-layouts: 11.1 us -> 13.3 us
  transfers between devices with their start and end apart: 19 -> 20, of which waited for: 14 -> 16; matrix products, arithmetic and copies ran while one was open for 2% -> 1% of each run, Pallas kernels for 5% -> 41%
where the time goes in v2:
time: 522 us
  Pallas kernels  279 us (53%)
  waiting for transfers between devices  184 us (35%)
  starting transfers between devices  24.2 us (5%)
  local copies, waits for them, and re-layouts  20.3 us (4%)
  between operations  13.5 us (3%)
    all_gather x2, waiting for transfers between devices, body(): got = lax.all_gather(cut, ('island', 'fsdp'), axis=0, tiled=False)  125 us
    pallas_call x2, Pallas kernels, pick(): pl.pallas_call(functools.partial(pick_kernel, part, tok), grid_spec=pltpu...  103 us
    pallas_call x8, Pallas kernels, last(): pl.pallas_call(functools.partial(last_kernel, 1.0 / math.sqrt(depth)), gr...  78.9 us
    pallas_call x1, Pallas kernels, middle(): pl.pallas_call(functools.partial(middle_kernel, 1.0 / math.sqrt(depth)),...  53.4 us
    ppermute x8, waiting for transfers between devices, body(): lax.ppermute(own, 'island', [(i, i ^ reach) for i in range(islands)])  32.2 us
    pallas_call x8, Pallas kernels, outer_update(): pl.pallas_call(functools.partial(sum_update_kernel, islands), grid_spec=p...  26.6 us
    ppermute x8, waiting for transfers between devices, body(): fresh.append(lax.ppermute(mine, 'island', partner))  26 us
    pallas_call x8, Pallas kernels, place(): pl.pallas_call(place_kernel, grid_spec=pltpu.PrefetchScalarGridSpec(num_s...  17.3 us
  transfers between devices with their start and end apart: 20, of which 16 were waited for; matrix products, arithmetic and copies ran while one was open for 1% of the time, Pallas kernels for 41%

profile of v2, /device:TPU:0, one launch (start us, length us, event | category | flops | bytes accessed | tf_op | source)
XLA Modules:
  0.0 521.8 jit_solution(4986305313491221791)
XLA Ops:
  6.5 1.8 constant_dynamic-slice_fusion
  9.2 3.0 collective-permute-start
  12.2 2.2 dynamic-slice_bitcast_fusion
  15.1 3.0 reshape.21.ids
  18.1 96.9 %all-gather.7.cloned.1.call-done = bf16[16384,256]{1,0:T(8,128)(2,1)} async-done(((bf16[512,256]{1,0:T(8,128)(2,1)}), bf16[16384,256]{1,0:T(8,128)(2,1)}) %all-gather.7.cloned.1.call-update) | async-done | bytes 8388624 | tf_op jit(solution)/shard_map/all_gather | solution.py:361
  115.0 50.9 %pick_0.1 = (bf16[2,2,2048,896]{3,2,1,0:T(8,128)(2,1)}, bf16[2,2,2048,896]{3,2,1,0:T(8,128)(2,1)}, f32[1792,896]{1,0:T(8,128)}) custom-call(s32[1]{0:T(128)} %bitcast.side, s32[3584,1]{1,0:T(8,128)} %reshape.21.ids, bf16[4,8,512,256]{3,2,1,0:T(8,128)(2,1)} %bitcast.14, bf16[4096,1792]{1,0:T(8,128)(2,1)} %weights.37), custom_call_target="tpu_custom_call" | custom-call | flops 36641439744 | bytes 50000000 | tf_op jit(solution)/shard_map/pick_0/pallas_call | solution.py:86
  165.9 27.9 %all-gather.5.cloned.1.call-done = bf16[16384,256]{1,0:T(8,128)(2,1)} async-done(((bf16[512,256]{1,0:T(8,128)(2,1)}), bf16[16384,256]{1,0:T(8,128)(2,1)}) %all-gather.5.cloned.1.call-update) | async-done | bytes 8388624 | tf_op jit(solution)/shard_map/all_gather | solution.py:361
  193.8 52.3 %pick_1.1 = (bf16[2,2,2048,896]{3,2,1,0:T(8,128)(2,1)}, bf16[2,2,2048,896]{3,2,1,0:T(8,128)(2,1)}, f32[1792,896]{1,0:T(8,128)}) custom-call(s32[1]{0:T(128)} %bitcast.side, s32[3584,1]{1,0:T(8,128)} %reshape.21.ids, bf16[4,8,512,256]{3,2,1,0:T(8,128)(2,1)} %bitcast.15, ...), custom_call_target="tpu_custom_call", output_to_operand_aliasing={{2}: (4, {}), {0}: (5, {}), {1}: (6, {})} | custom-call | flops 36641439744 | bytes 50000000 | tf_op jit(solution)/shard_map/pick_1/pallas_call | solution.py:86
  246.1 53.4 %middle.1 = (bf16[2,2,2048,896]{3,2,1,0:T(8,128)(2,1)}, bf16[1792,896]{1,0:T(8,128)(2,1)}) custom-call(s32[1]{0:T(128)} %bitcast.side, f32[1792,896]{1,0:T(8,128)} %get-tuple-element.33.hidden, bf16[2,896,1792]{2,1,0:T(8,128)(2,1)} %bitcast.9, bf16[2,896,896]{2,1,0:T(8,128)(2,1)} %collective-permute-done.1.other.other_late, ...), custom_call_target="tpu_custom_call", output_to_operand_aliasing={{0}: (6, {})} | custom-call | flops 26306674688 | bytes 90000000 | tf_op jit(solution)/shard_map/middle/pallas_call | solution.py:173
  299.4 9.8 %last_0.1.own = bf16[512,896]{1,0:T(8,128)(2,1)} custom-call(s32[1]{0:T(128)} %bitcast.side, bf16[2,2,2048,896]{3,2,1,0:T(8,128)(2,1)} %get-tuple-element.32.late, bf16[1792,896]{1,0:T(8,128)(2,1)} %get-tuple-element.35.upstream, bf16[2,2,2048,896]{3,2,1,0:T(8,128)(2,1)} %get-tuple-element.36.grad_one, bf16[4096,1792]{1,0:T(8,128)(2,1)} %weights.37), custom_call_target="tpu_custom_call" | custom-call | flops 1644167168 | bytes 10000000 | tf_op jit(solution)/shard_map/last_0/pallas_call | solution.py:242
  309.3 1.5 collective-permute-start.3
  310.7 9.9 %last_1.1.own = bf16[512,896]{1,0:T(8,128)(2,1)} custom-call(s32[1]{0:T(128)} %bitcast.side, bf16[2,2,2048,896]{3,2,1,0:T(8,128)(2,1)} %get-tuple-element.32.late, bf16[1792,896]{1,0:T(8,128)(2,1)} %get-tuple-element.35.upstream, bf16[2,2,2048,896]{3,2,1,0:T(8,128)(2,1)} %get-tuple-element.36.grad_one, bf16[4096,1792]{1,0:T(8,128)(2,1)} %weights.37), custom_call_target="tpu_custom_call" | custom-call | flops 1644167168 | bytes 10000000 | tf_op jit(solution)/shard_map/last_1/pallas_call | solution.py:242
  321.2 11.4 %collective-permute-done.3.other.refs_0_ = bf16[512,896]{1,0:T(8,128)(2,1)S(1)} collective-permute-done((bf16[512,896]{1,0:T(8,128)(2,1)}, bf16[512,896]{1,0:T(8,128)(2,1)S(1)}, u32[]{:S(2)}, u32[]{:S(2)}) %collective-permute-start.3) | collective-permute-done | bytes 917536 | tf_op jit(solution)/shard_map/ppermute | solution.py:394
  333.6 3.3 outer_update_0.1
  336.9 1.4 collective-permute-start.4
  338.3 9.9 %last_2.1.own = bf16[512,896]{1,0:T(8,128)(2,1)} custom-call(s32[1]{0:T(128)} %bitcast.side, bf16[2,2,2048,896]{3,2,1,0:T(8,128)(2,1)} %get-tuple-element.32.late, bf16[1792,896]{1,0:T(8,128)(2,1)} %get-tuple-element.35.upstream, bf16[2,2,2048,896]{3,2,1,0:T(8,128)(2,1)} %get-tuple-element.36.grad_one, bf16[4096,1792]{1,0:T(8,128)(2,1)} %weights.37, ...), custom_call_target="tpu_custom_call" | custom-call | flops 1644167168 | bytes 10000000 | tf_op jit(solution)/shard_map/last_2/pallas_call | solution.py:242
  348.8 3.5 collective-permute-done.2.refs_0_.other
  352.3 1.0 copy-done.8
  353.3 3.3 outer_update_1.1
  356.6 1.4 collective-permute-start.9
  358.2 1.0 copy-done
  359.1 9.9 %last_3.1.own = bf16[512,896]{1,0:T(8,128)(2,1)} custom-call(s32[1]{0:T(128)} %bitcast.side, bf16[2,2,2048,896]{3,2,1,0:T(8,128)(2,1)} %get-tuple-element.32.late, bf16[1792,896]{1,0:T(8,128)(2,1)} %get-tuple-element.35.upstream, bf16[2,2,2048,896]{3,2,1,0:T(8,128)(2,1)} %get-tuple-element.36.grad_one, bf16[4096,1792]{1,0:T(8,128)(2,1)} %weights.37, ...), custom_call_target="tpu_custom_call" | custom-call | flops 1644167168 | bytes 10000000 | tf_op jit(solution)/shard_map/last_3/pallas_call | solution.py:242
  369.0 1.5 collective-permute-start.5
  370.5 1.5 collective-permute-done.6.other.refs_0_
  372.0 1.0 copy-done.6
  372.9 3.3 outer_update_2.1
  376.3 1.4 collective-permute-start.7
  378.8 9.8 %last_4.1.own = bf16[512,896]{1,0:T(8,128)(2,1)} custom-call(s32[1]{0:T(128)} %bitcast.side, bf16[2,2,2048,896]{3,2,1,0:T(8,128)(2,1)} %get-tuple-element.32.late, bf16[1792,896]{1,0:T(8,128)(2,1)} %get-tuple-element.35.upstream, bf16[2,2,2048,896]{3,2,1,0:T(8,128)(2,1)} %get-tuple-element.36.grad_one, bf16[4096,1792]{1,0:T(8,128)(2,1)} %weights.37, ...), custom_call_target="tpu_custom_call" | custom-call | flops 1644167168 | bytes 10000000 | tf_op jit(solution)/shard_map/last_4/pallas_call | solution.py:242
  388.6 1.5 collective-permute-start.10
  390.1 2.0 collective-permute-done.5.refs_0_.other
  392.1 1.0 copy-done.7
  393.0 3.3 outer_update_3.1
  396.4 1.8 collective-permute-start.13
  399.2 9.9 %last_5.1.own = bf16[512,896]{1,0:T(8,128)(2,1)} custom-call(s32[1]{0:T(128)} %bitcast.side, bf16[2,2,2048,896]{3,2,1,0:T(8,128)(2,1)} %get-tuple-element.32.late, bf16[1792,896]{1,0:T(8,128)(2,1)} %get-tuple-element.35.upstream, bf16[2,2,2048,896]{3,2,1,0:T(8,128)(2,1)} %get-tuple-element.36.grad_one, bf16[4096,1792]{1,0:T(8,128)(2,1)} %weights.37, ...), custom_call_target="tpu_custom_call" | custom-call | flops 1644167168 | bytes 10000000 | tf_op jit(solution)/shard_map/last_5/pallas_call | solution.py:242
  409.1 1.5 collective-permute-start.8
  410.6 1.7 collective-permute-done.10.other.refs_0_
  412.2 3.4 outer_update_4.1
  415.6 1.4 collective-permute-start.11
  417.0 1.7 collective-permute-done.13.refs_1_.block
  419.7 9.8 %last_6.1.own = bf16[512,896]{1,0:T(8,128)(2,1)} custom-call(s32[1]{0:T(128)} %bitcast.side, bf16[2,2,2048,896]{3,2,1,0:T(8,128)(2,1)} %get-tuple-element.32.late, bf16[1792,896]{1,0:T(8,128)(2,1)} %get-tuple-element.35.upstream, bf16[2,2,2048,896]{3,2,1,0:T(8,128)(2,1)} %get-tuple-element.36.grad_one, bf16[4096,1792]{1,0:T(8,128)(2,1)} %weights.37, ...), custom_call_target="tpu_custom_call" | custom-call | flops 1644167168 | bytes 10000000 | tf_op jit(solution)/shard_map/last_6/pallas_call | solution.py:242
  429.5 1.5 collective-permute-start.14
  431.0 1.3 collective-permute-done.8.refs_0_.other
  432.3 4.5 collective-permute-done.11.refs_1_.block
  436.8 1.0 copy-done.4
  437.8 9.9 %last_7.1.own = bf16[512,896]{1,0:T(8,128)(2,1)} custom-call(s32[1]{0:T(128)} %bitcast.side, bf16[2,2,2048,896]{3,2,1,0:T(8,128)(2,1)} %get-tuple-element.32.late, bf16[1792,896]{1,0:T(8,128)(2,1)} %get-tuple-element.35.upstream, bf16[2,2,2048,896]{3,2,1,0:T(8,128)(2,1)} %get-tuple-element.36.grad_one, bf16[4096,1792]{1,0:T(8,128)(2,1)} %weights.37, ...), custom_call_target="tpu_custom_call" | custom-call | flops 1644167168 | bytes 10000000 | tf_op jit(solution)/shard_map/last_7/pallas_call | solution.py:242
  447.7 1.5 collective-permute-start.12
  449.2 3.3 outer_update_5.1
  454.0 3.3 outer_update_6.1
  457.3 1.5 collective-permute-start.16
  458.8 10.8 %collective-permute-done.12.other = bf16[512,896]{1,0:T(8,128)(2,1)S(1)} collective-permute-done((bf16[512,896]{1,0:T(8,128)(2,1)}, bf16[512,896]{1,0:T(8,128)(2,1)S(1)}, u32[]{:S(2)}, u32[]{:S(2)}) %collective-permute-start.12) | collective-permute-done | bytes 917536 | tf_op jit(solution)/shard_map/ppermute | solution.py:394
  470.6 3.3 outer_update_7.1
  473.9 1.4 collective-permute-start.15
  475.3 2.2 place_0.1.held
  477.5 2.2 place_1.1.held
  479.7 2.2 place_2.1.held
  481.8 2.2 place_3.1.held
  484.0 2.2 place_4.1.held
  486.2 1.0 copy-done.10
  487.1 2.2 place_5.1.held
  489.3 6.3 %collective-permute-done.16.block = bf16[512,896]{1,0:T(8,128)(2,1)S(1)} collective-permute-done((bf16[512,896]{1,0:T(8,128)(2,1)}, bf16[512,896]{1,0:T(8,128)(2,1)S(1)}, u32[]{:S(2)}, u32[]{:S(2)}) %collective-permute-start.16) | collective-permute-done | bytes 917536 | tf_op jit(solution)/shard_map/ppermute | solution.py:404
  495.6 1.0 copy-done.11
  496.6 2.2 place_6.1.held
  498.8 13.0 %collective-permute-done.15.block = bf16[512,896]{1,0:T(8,128)(2,1)S(1)} collective-permute-done((bf16[512,896]{1,0:T(8,128)(2,1)}, bf16[512,896]{1,0:T(8,128)(2,1)S(1)}, u32[]{:S(2)}, u32[]{:S(2)}) %collective-permute-start.15) | collective-permute-done | bytes 917536 | tf_op jit(solution)/shard_map/ppermute | solution.py:404
  512.8 2.2 place_7.1
  (40 shorter events, 10.3 us)
Async XLA Ops:
  6.5 108.5 %all-gather.7.cloned.1.call-start = ((), (), s32[]{:S(2)}) async-start(), calls=%async_computation.1 | async-start | bytes 8650752 | tf_op jit(solution)/shard_map/all_gather | solution.py:361
  8.4 185.4 %all-gather.5.cloned.1.call-start = ((), (), s32[]{:S(2)}) async-start(), calls=%async_computation | async-start | bytes 8650752 | tf_op jit(solution)/shard_map/all_gather | solution.py:361
  9.2 5.3 %collective-permute-start = (s32[2,896]{1,0:T(2,128)}, s32[2,896]{1,0:T(2,128)S(1)}, u32[]{:S(2)}, u32[]{:S(2)}) collective-permute-start(s32[2,896]{1,0:T(2,128)} %bitcast.11), channel_id=1, source_target_pairs={{0,8},{8,0},{16,24},{24,16},{1,9},{9,1},{17,25},{25,17},{2,10},{10... | collective-permute-start | bytes 21512 | tf_op jit(solution)/shard_map/ppermute | solution.py:365
  14.3 231.7 %collective-permute-start.1 = (bf16[2,896,896]{2,1,0:T(8,128)(2,1)S(1)}, bf16[2,896,896]{2,1,0:T(8,128)(2,1)}, u32[]{:S(2)}, u32[]{:S(2)}) collective-permute-start(bf16[2,896,896]{2,1,0:T(8,128)(2,1)S(1)} %dynamic-slice_bitcast_fusion), channel_id=1, source_target_pairs={{0,8},{8,0},{16,24},{24,16},{1,9},{9,1},{17,25},{25,17},{2,10},{10... | collective-permute-start | bytes 9633800 | tf_op jit(solution)/shard_map/ppermute | solution.py:367
  309.3 23.4 %collective-permute-start.3 = (bf16[512,896]{1,0:T(8,128)(2,1)}, bf16[512,896]{1,0:T(8,128)(2,1)S(1)}, u32[]{:S(2)}, u32[]{:S(2)}) collective-permute-start(bf16[512,896]{1,0:T(8,128)(2,1)} %last_0.1.own), channel_id=1, source_target_pairs={{0,16},{8,24},{16,0},{24,8},{1,17},{9,25},{17,1},{25,9},{2,18},{10... | collective-permute-start | bytes 2752520 | tf_op jit(solution)/shard_map/ppermute | solution.py:394
  320.7 31.6 %collective-permute-start.2 = (bf16[512,896]{1,0:T(8,128)(2,1)}, bf16[512,896]{1,0:T(8,128)(2,1)S(1)}, u32[]{:S(2)}, u32[]{:S(2)}) collective-permute-start(bf16[512,896]{1,0:T(8,128)(2,1)} %last_1.1.own), channel_id=1, source_target_pairs={{0,16},{8,24},{16,0},{24,8},{1,17},{9,25},{17,1},{25,9},{2,18},{10... | collective-permute-start | bytes 2752520 | tf_op jit(solution)/shard_map/ppermute | solution.py:394
  332.6 0.9 copy-start.9
  336.9 21.2 %collective-permute-start.4 = (bf16[512,896]{1,0:T(8,128)(2,1)}, bf16[512,896]{1,0:T(8,128)(2,1)S(1)}, u32[]{:S(2)}, u32[]{:S(2)}) collective-permute-start(bf16[512,896]{1,0:T(8,128)(2,1)} %get-tuple-element.37), channel_id=1, source_target_pairs={{0,8},{8,0},{16,24},{24,16},{1,9},{9,1},{17,25},{25,17},{2,10},{10... | collective-permute-start | bytes 2752520 | tf_op jit(solution)/shard_map/ppermute | solution.py:404
  348.2 23.8 %collective-permute-start.6 = (bf16[512,896]{1,0:T(8,128)(2,1)}, bf16[512,896]{1,0:T(8,128)(2,1)S(1)}, u32[]{:S(2)}, u32[]{:S(2)}) collective-permute-start(bf16[512,896]{1,0:T(8,128)(2,1)} %last_2.1.own), channel_id=1, source_target_pairs={{0,16},{8,24},{16,0},{24,8},{1,17},{9,25},{17,1},{25,9},{2,18},{10... | collective-permute-start | bytes 2752520 | tf_op jit(solution)/shard_map/ppermute | solution.py:394
  352.3 1.0 copy-start.8
  356.6 21.2 %collective-permute-start.9 = (bf16[512,896]{1,0:T(8,128)(2,1)}, bf16[512,896]{1,0:T(8,128)(2,1)S(1)}, u32[]{:S(2)}, u32[]{:S(2)}) collective-permute-start(bf16[512,896]{1,0:T(8,128)(2,1)} %get-tuple-element.41), channel_id=1, source_target_pairs={{0,8},{8,0},{16,24},{24,16},{1,9},{9,1},{17,25},{25,17},{2,10},{10... | collective-permute-start | bytes 2752520 | tf_op jit(solution)/shard_map/ppermute | solution.py:404
  358.2 1.0 copy-start
  369.0 23.1 %collective-permute-start.5 = (bf16[512,896]{1,0:T(8,128)(2,1)}, bf16[512,896]{1,0:T(8,128)(2,1)S(1)}, u32[]{:S(2)}, u32[]{:S(2)}) collective-permute-start(bf16[512,896]{1,0:T(8,128)(2,1)} %last_3.1.own), channel_id=1, source_target_pairs={{0,16},{8,24},{16,0},{24,8},{1,17},{9,25},{17,1},{25,9},{2,18},{10... | collective-permute-start | bytes 2752520 | tf_op jit(solution)/shard_map/ppermute | solution.py:394
  372.0 1.0 copy-start.6
  376.3 22.0 %collective-permute-start.7 = (bf16[512,896]{1,0:T(8,128)(2,1)}, bf16[512,896]{1,0:T(8,128)(2,1)S(1)}, u32[]{:S(2)}, u32[]{:S(2)}) collective-permute-start(bf16[512,896]{1,0:T(8,128)(2,1)} %get-tuple-element.40), channel_id=1, source_target_pairs={{0,8},{8,0},{16,24},{24,16},{1,9},{9,1},{17,25},{25,17},{2,10},{10... | collective-permute-start | bytes 2752520 | tf_op jit(solution)/shard_map/ppermute | solution.py:404
  377.8 0.9 copy-start.1
  388.6 23.6 %collective-permute-start.10 = (bf16[512,896]{1,0:T(8,128)(2,1)}, bf16[512,896]{1,0:T(8,128)(2,1)}, u32[]{:S(2)}, u32[]{:S(2)}) collective-permute-start(bf16[512,896]{1,0:T(8,128)(2,1)} %last_4.1.own), channel_id=1, source_target_pairs={{0,16},{8,24},{16,0},{24,8},{1,17},{9,25},{17,1},{25,9},{2,18},{10... | collective-permute-start | bytes 2752520 | tf_op jit(solution)/shard_map/ppermute | solution.py:394
  392.1 1.0 copy-start.7
  396.4 22.4 %collective-permute-start.13 = (bf16[512,896]{1,0:T(8,128)(2,1)}, bf16[512,896]{1,0:T(8,128)(2,1)S(1)}, u32[]{:S(2)}, u32[]{:S(2)}) collective-permute-start(bf16[512,896]{1,0:T(8,128)(2,1)} %get-tuple-element.45), channel_id=1, source_target_pairs={{0,8},{8,0},{16,24},{24,16},{1,9},{9,1},{17,25},{25,17},{2,10},{10... | collective-permute-start | bytes 2752520 | tf_op jit(solution)/shard_map/ppermute | solution.py:404
  398.3 0.9 copy-start.2
  409.1 23.3 %collective-permute-start.8 = (bf16[512,896]{1,0:T(8,128)(2,1)}, bf16[512,896]{1,0:T(8,128)(2,1)S(1)}, u32[]{:S(2)}, u32[]{:S(2)}) collective-permute-start(bf16[512,896]{1,0:T(8,128)(2,1)} %last_5.1.own), channel_id=1, source_target_pairs={{0,16},{8,24},{16,0},{24,8},{1,17},{9,25},{17,1},{25,9},{2,18},{10... | collective-permute-start | bytes 2752520 | tf_op jit(solution)/shard_map/ppermute | solution.py:394
  415.6 21.2 %collective-permute-start.11 = (bf16[512,896]{1,0:T(8,128)(2,1)}, bf16[512,896]{1,0:T(8,128)(2,1)S(1)}, u32[]{:S(2)}, u32[]{:S(2)}) collective-permute-start(bf16[512,896]{1,0:T(8,128)(2,1)} %get-tuple-element.44), channel_id=1, source_target_pairs={{0,8},{8,0},{16,24},{24,16},{1,9},{9,1},{17,25},{25,17},{2,10},{10... | collective-permute-start | bytes 2752520 | tf_op jit(solution)/shard_map/ppermute | solution.py:404
  418.8 0.9 copy-start.3
  429.5 23.5 %collective-permute-start.14 = (bf16[512,896]{1,0:T(8,128)(2,1)}, bf16[512,896]{1,0:T(8,128)(2,1)S(1)}, u32[]{:S(2)}, u32[]{:S(2)}) collective-permute-start(bf16[512,896]{1,0:T(8,128)(2,1)} %last_6.1.own), channel_id=1, source_target_pairs={{0,16},{8,24},{16,0},{24,8},{1,17},{9,25},{17,1},{25,9},{2,18},{10... | collective-permute-start | bytes 2752520 | tf_op jit(solution)/shard_map/ppermute | solution.py:394
  432.3 4.5 copy-start.5
  436.8 1.0 copy-start.4
  447.7 21.9 %collective-permute-start.12 = (bf16[512,896]{1,0:T(8,128)(2,1)}, bf16[512,896]{1,0:T(8,128)(2,1)S(1)}, u32[]{:S(2)}, u32[]{:S(2)}) collective-permute-start(bf16[512,896]{1,0:T(8,128)(2,1)} %last_7.1.own), channel_id=1, source_target_pairs={{0,16},{8,24},{16,0},{24,8},{1,17},{9,25},{17,1},{25,9},{2,18},{10... | collective-permute-start | bytes 2752520 | tf_op jit(solution)/shard_map/ppermute | solution.py:394
  452.5 33.7 %collective-permute-start.17 = (bf16[512,896]{1,0:T(8,128)(2,1)}, bf16[512,896]{1,0:T(8,128)(2,1)S(1)}, u32[]{:S(2)}, u32[]{:S(2)}) collective-permute-start(bf16[512,896]{1,0:T(8,128)(2,1)} %get-tuple-element.51), channel_id=1, source_target_pairs={{0,8},{8,0},{16,24},{24,16},{1,9},{9,1},{17,25},{25,17},{2,10},{10... | collective-permute-start | bytes 2752520 | tf_op jit(solution)/shard_map/ppermute | solution.py:404
  453.1 0.9 copy-start.13
  457.3 38.3 %collective-permute-start.16 = (bf16[512,896]{1,0:T(8,128)(2,1)}, bf16[512,896]{1,0:T(8,128)(2,1)S(1)}, u32[]{:S(2)}, u32[]{:S(2)}) collective-permute-start(bf16[512,896]{1,0:T(8,128)(2,1)} %get-tuple-element.50), channel_id=1, source_target_pairs={{0,8},{8,0},{16,24},{24,16},{1,9},{9,1},{17,25},{25,17},{2,10},{10... | collective-permute-start | bytes 2752520 | tf_op jit(solution)/shard_map/ppermute | solution.py:404
  469.6 0.9 copy-start.14
  473.9 37.9 %collective-permute-start.15 = (bf16[512,896]{1,0:T(8,128)(2,1)}, bf16[512,896]{1,0:T(8,128)(2,1)S(1)}, u32[]{:S(2)}, u32[]{:S(2)}) collective-permute-start(bf16[512,896]{1,0:T(8,128)(2,1)} %get-tuple-element.49), channel_id=1, source_target_pairs={{0,8},{8,0},{16,24},{24,16},{1,9},{9,1},{17,25},{25,17},{2,10},{10... | collective-permute-start | bytes 2752520 | tf_op jit(solution)/shard_map/ppermute | solution.py:404
  486.2 1.0 copy-start.10
  495.6 1.0 copy-start.11
  511.8 1.0 copy-start.12
Sparse Core Ops, SparseCore 0:
  10.3 104.6 all-gather.6
  118.0 75.7 all-gather.4

commit v3 on v2

--- a/solution.py
+++ b/solution.py
@@ -125,8 +125,7 @@
 
 
 def middle_kernel(
-    scale, side, hidden, own, other, own_late, other_late, early, late, weights,
-    grad_one, upstream_late, upstream, hidden_late,
+    scale, side, hidden, own, other, early, late, weights, grad_one, hidden_late, upstream
 ):
     tok = own.shape[0]
     parts, part = early.shape[1:3]
@@ -153,10 +152,6 @@
                 late[island, index].T, work, preferred_element_type=jnp.float32
             )
 
-    @pl.when(at == pl.num_programs(0) - 1)
-    def _():
-        make_upstream(hidden_late, (own_late, other_late), scale, upstream_late)
-
 
 def middle(tiles, column, side, hidden, cot, cot_other, early, late, weights):
     double, half = hidden.shape
@@ -165,10 +160,6 @@
     parts = early.shape[1]
     part = early.shape[2] // tiles
     once = pl.Buffered(1)
-    cot_spec = lambda step, side_of: pl.BlockSpec(
-        (None, tok, half), lambda at, side: (step, 0, side_of(side)), pipeline_mode=once
-    )
-    none = lambda side: 0
     tall = lambda width: pl.BlockSpec((2, parts, part, width), lambda at, side: (0, 0, at, 0))
     return pl.pallas_call(
         functools.partial(middle_kernel, 1.0 / math.sqrt(depth)),
@@ -177,10 +168,10 @@
             grid=(tiles,),
             in_specs=[
                 pl.BlockSpec((double, half), lambda at, side: (0, 0), pipeline_mode=once),
-                cot_spec(0, column),
-                cot_spec(0, none),
-                cot_spec(1, column),
-                cot_spec(1, none),
+                pl.BlockSpec(
+                    (None, tok, half), lambda at, side: (0, 0, column(side)), pipeline_mode=once
+                ),
+                pl.BlockSpec((tok, half), lambda at, side: (0, 0), pipeline_mode=once),
                 tall(tok),
                 tall(tok),
                 pl.BlockSpec((parts * part, half), lambda at, side: (at, column(side))),
@@ -191,20 +182,75 @@
             ],
             scratch_shapes=[
                 pltpu.VMEM((double, half), jnp.bfloat16),
-                pltpu.VMEM((double, half), jnp.float32),
             ],
         ),
         out_shape=[
             jax.ShapeDtypeStruct(early.shape[:3] + (half,), jnp.bfloat16),
-            jax.ShapeDtypeStruct((double, half), jnp.bfloat16),
+            jax.ShapeDtypeStruct((double, half), jnp.float32),
         ],
-        input_output_aliases={6: 0} if tok == half else {},
+        input_output_aliases={4: 0} if tok == half else {},
         compiler_params=params(60),
         cost_estimate=pl.CostEstimate(
             flops=2 * 2 * double * depth * half, bytes_accessed=90_000_000, transcendentals=0
         ),
         name="middle",
-    )(side, hidden, cot, cot_other, cot, cot_other, early, late, weights)
+    )(side, hidden, cot, cot_other, early, late, weights)
+
+
+def upstream_kernel(scale, side, hidden, own, other, upstream):
+    make_upstream(hidden, (own, other), scale, upstream)
+
+
+def upstream_of(step, depth, column, side, hidden, cot, cot_other):
+    double, half = hidden.shape
+    tok = double // 2
+    whole = lambda shape: pl.BlockSpec(shape, lambda at, side: (0, 0))
+    return pl.pallas_call(
+        functools.partial(upstream_kernel, 1.0 / math.sqrt(depth)),
+        grid_spec=pltpu.PrefetchScalarGridSpec(
+            num_scalar_prefetch=1,
+            grid=(1,),
+            in_specs=[
+                whole((double, half)),
+                pl.BlockSpec((None, tok, half), lambda at, side: (step, 0, column(side))),
+                whole((tok, half)),
+            ],
+            out_specs=whole((double, half)),
+        ),
+        out_shape=jax.ShapeDtypeStruct((double, half), jnp.bfloat16),
+        compiler_params=params(60),
+        cost_estimate=pl.CostEstimate(
+            flops=30 * double * half, bytes_accessed=10 * double * half, transcendentals=0
+        ),
+        name="upstream",
+    )(side, hidden, cot, cot_other)
+
+
+def cut_kernel(side, cot, after, out):
+    out[...] = cot[...]
+
+
+def cut(step, side, cot, after):
+    tok, columns = cot.shape[1:]
+    half = columns // 2
+    return pl.pallas_call(
+        cut_kernel,
+        grid_spec=pltpu.PrefetchScalarGridSpec(
+            num_scalar_prefetch=1,
+            grid=(2,),
+            in_specs=[
+                pl.BlockSpec((None, tok // 2, half), lambda at, side: (step, at, 1 - side[0])),
+                pl.BlockSpec(memory_space=pl.ANY),
+            ],
+            out_specs=pl.BlockSpec((tok // 2, half), lambda at, side: (at, 0)),
+        ),
+        out_shape=jax.ShapeDtypeStruct((tok, half), cot.dtype),
+        compiler_params=params(60),
+        cost_estimate=pl.CostEstimate(
+            flops=0, bytes_accessed=4 * tok * half, transcendentals=0
+        ),
+        name=f"cut_{step}",
+    )(side, cot, after)
 
 
 def last_kernel(scale, side, late, upstream, grad_one, weights, *refs):
@@ -357,31 +403,40 @@
     mine = lax.dynamic_slice_in_dim(table, me * quarter, quarter, 0)
     pieces = []
     for part in range(parts):
-        cut = lax.slice_in_dim(mine, part * feat // parts, (part + 1) * feat // parts, axis=1)
-        got = lax.all_gather(cut, ("island", "fsdp"), axis=0, tiled=False)
+        share = lax.slice_in_dim(mine, part * feat // parts, (part + 1) * feat // parts, axis=1)
+        got = lax.all_gather(share, ("island", "fsdp"), axis=0, tiled=False)
         pieces.append(got.reshape(islands, shards, quarter, feat // parts))
 
     cot = cotangent[0]
     ids_other = lax.ppermute(token_ids[0], "island", partner)
-    to_send = lax.dynamic_slice_in_dim(cot, (1 - side[0]) * half, half, 2)
-    cot_other = lax.ppermute(to_send, "island", partner)
     ids = jnp.stack([token_ids[0], ids_other], axis=1)
 
     steps, tok = token_ids.shape[1:]
     aligned = half % 128 == 0
+    whole_cot = cot
+
+    def partners(step, after):
+        if aligned:
+            sent = cut(step, side, whole_cot, after)
+        else:
+            sent = take_half(whole_cot[step], 1 - side[0], half)
+        return lax.ppermute(sent, "island", partner)
+
     if not aligned:
         cot, weights, momentum = (take_half(a, side[0], half) for a in (cot, weights, momentum))
     column = (lambda side: side[0]) if aligned else (lambda side: 0)
     ids = ids.reshape(2 * steps * tok, 1)
-    behind = []
+    behind, cot_other = [], []
     for part in range(parts):
         early, late, hidden = pick(
             part, parts, column, side, ids, pieces[part], weights, half, behind
         )
         behind = [hidden, early, late]
-    grad_one, upstream = middle(
-        shards, column, side, hidden, cot, cot_other, early, late, weights
+        cot_other.append(partners(part, hidden))
+    grad_one, hidden_late = middle(
+        shards, column, side, hidden, cot, cot_other[0], early, late, weights
     )
+    upstream = upstream_of(1, depth, column, side, hidden_late, cot, cot_other[1])
 
     held = None
     size = depth // CHUNKS

time: 522 us -> 532 us (1.019)
  Pallas kernels: 279 us -> 290 us
    all_gather x2, waiting for transfers between devices: 125 us -> 106 us  [body(): got = lax.all_gather(share, ('island', 'fsdp'), axis=0, tiled=False)]
    pallas_call x0 -> x3, Pallas kernels: none -> 12.7 us  [the longest x1 7.9 us: upstream_of(): pl.pallas_call(functools.partial(upstream_kernel, 1.0 / math.sqrt(depth))...]
    ppermute x8, waiting for transfers between devices: 26 us -> 34.2 us  [body(): fresh.append(lax.ppermute(mine, 'island', partner))]
    ppermute x8, waiting for transfers between devices: 32.2 us -> 38.9 us  [body(): lax.ppermute(own, 'island', [(i, i ^ reach) for i in range(islands)])]
    unnamed x30 -> x36, local copies, waits for them, and re-layouts: 13.3 us -> 16.7 us
  transfers between devices with their start and end apart: 20 -> 21, of which waited for: 16 -> 15; matrix products, arithmetic and copies ran while one was open for 1% -> 1% of each run, Pallas kernels for 41% -> 51%
where the time goes in v3:
time: 532 us; the launch traced here: 531 us
  Pallas kernels  290 us (55%)
  waiting for transfers between devices  182 us (34%)
  starting transfers between devices  24.2 us (5%)
  local copies, waits for them, and re-layouts  21.6 us (4%)
  between operations  13.5 us (3%)
    all_gather x2, waiting for transfers between devices, body(): got = lax.all_gather(share, ('island', 'fsdp'), axis=0, tiled=False)  106 us
    pallas_call x2, Pallas kernels, pick(): pl.pallas_call(functools.partial(pick_kernel, part, tok), grid_spec=pltpu...  103 us
    pallas_call x8, Pallas kernels, last(): pl.pallas_call(functools.partial(last_kernel, 1.0 / math.sqrt(depth)), gr...  79.1 us
    pallas_call x1, Pallas kernels, middle(): pl.pallas_call(functools.partial(middle_kernel, 1.0 / math.sqrt(depth)),...  50.6 us
    ppermute x8, waiting for transfers between devices, body(): lax.ppermute(own, 'island', [(i, i ^ reach) for i in range(islands)])  38.9 us
    ppermute x8, waiting for transfers between devices, body(): fresh.append(lax.ppermute(mine, 'island', partner))  34.2 us
    pallas_call x8, Pallas kernels, outer_update(): pl.pallas_call(functools.partial(sum_update_kernel, islands), grid_spec=p...  26.7 us
    pallas_call x8, Pallas kernels, place(): pl.pallas_call(place_kernel, grid_spec=pltpu.PrefetchScalarGridSpec(num_s...  17.3 us
  transfers between devices with their start and end apart: 21, of which 15 were waited for; matrix products, arithmetic and copies ran while one was open for 1% of the time, Pallas kernels for 51%

profile of v3, /device:TPU:0, one launch (start us, length us, event | category | flops | bytes accessed | tf_op | source)
XLA Modules:
  0.0 531.1 jit_solution(236375527193374744)
XLA Ops:
  6.5 1.8 constant_dynamic-slice_fusion
  9.2 3.0 collective-permute-start
  12.2 1.8 collective-permute-done
  14.7 3.0 reshape.20.ids
  17.7 72.8 %all-gather.7.cloned.1.call-done = bf16[16384,256]{1,0:T(8,128)(2,1)} async-done(((bf16[512,256]{1,0:T(8,128)(2,1)}), bf16[16384,256]{1,0:T(8,128)(2,1)}) %all-gather.7.cloned.1.call-update) | async-done | bytes 8388624 | tf_op jit(solution)/shard_map/all_gather | solution.py:407
  90.5 50.9 %pick_0.1 = (bf16[2,2,2048,896]{3,2,1,0:T(8,128)(2,1)}, bf16[2,2,2048,896]{3,2,1,0:T(8,128)(2,1)}, f32[1792,896]{1,0:T(8,128)}) custom-call(s32[1]{0:T(128)} %bitcast.side, s32[3584,1]{1,0:T(8,128)} %reshape.20.ids, bf16[4,8,512,256]{3,2,1,0:T(8,128)(2,1)} %bitcast.15, bf16[4096,1792]{1,0:T(8,128)(2,1)} %weights.37), custom_call_target="tpu_custom_call" | custom-call | flops 36641439744 | bytes 50000000 | tf_op jit(solution)/shard_map/pick_0/pallas_call | solution.py:86
  141.4 2.4 cut_0.1
  143.7 1.4 collective-permute-start.1
  145.1 33.2 %all-gather.5.cloned.1.call-done = bf16[16384,256]{1,0:T(8,128)(2,1)} async-done(((bf16[512,256]{1,0:T(8,128)(2,1)}), bf16[16384,256]{1,0:T(8,128)(2,1)}) %all-gather.5.cloned.1.call-update) | async-done | bytes 8388624 | tf_op jit(solution)/shard_map/all_gather | solution.py:407
  178.3 52.3 %pick_1.1 = (bf16[2,2,2048,896]{3,2,1,0:T(8,128)(2,1)}, bf16[2,2,2048,896]{3,2,1,0:T(8,128)(2,1)}, f32[1792,896]{1,0:T(8,128)}) custom-call(s32[1]{0:T(128)} %bitcast.side, s32[3584,1]{1,0:T(8,128)} %reshape.20.ids, bf16[4,8,512,256]{3,2,1,0:T(8,128)(2,1)} %bitcast.14, ...), custom_call_target="tpu_custom_call", output_to_operand_aliasing={{2}: (4, {}), {0}: (5, {}), {1}: (6, {})} | custom-call | flops 36641439744 | bytes 50000000 | tf_op jit(solution)/shard_map/pick_1/pallas_call | solution.py:86
  230.6 2.4 cut_1.1
  233.0 1.2 copy-done.17
  234.2 50.6 %middle.1 = (bf16[2,2,2048,896]{3,2,1,0:T(8,128)(2,1)}, f32[1792,896]{1,0:T(8,128)}) custom-call(s32[1]{0:T(128)} %bitcast.side, f32[1792,896]{1,0:T(8,128)} %get-tuple-element.33.hidden.after, bf16[2,896,1792]{2,1,0:T(8,128)(2,1)} %bitcast.9, bf16[896,896]{1,0:T(8,128)(2,1)} %copy-done.17, ...), custom_call_target="tpu_custom_call", output_to_operand_aliasing={{0}: (4, {})} | custom-call | flops 26306674688 | bytes 90000000 | tf_op jit(solution)/shard_map/middle/pallas_call | solution.py:164
  284.8 1.1 copy-done.11
  286.0 7.9 %upstream.1 = bf16[1792,896]{1,0:T(8,128)(2,1)} custom-call(s32[1]{0:T(128)} %bitcast.side, f32[1792,896]{1,0:T(8,128)} %get-tuple-element.35.hidden, bf16[2,896,1792]{2,1,0:T(8,128)(2,1)} %bitcast.10, bf16[896,896]{1,0:T(8,128)(2,1)} %copy-done.11), custom_call_target="tpu_custom_call" | custom-call | flops 48168960 | bytes 16056320 | tf_op jit(solution)/shard_map/upstream/pallas_call | solution.py:208
  293.9 9.9 %last_0.1.own = bf16[512,896]{1,0:T(8,128)(2,1)} custom-call(s32[1]{0:T(128)} %bitcast.side, bf16[2,2,2048,896]{3,2,1,0:T(8,128)(2,1)} %get-tuple-element.32.late, bf16[1792,896]{1,0:T(8,128)(2,1)} %upstream.1, bf16[2,2,2048,896]{3,2,1,0:T(8,128)(2,1)} %get-tuple-element.36.grad_one, bf16[4096,1792]{1,0:T(8,128)(2,1)} %weights.37), custom_call_target="tpu_custom_call" | custom-call | flops 1644167168 | bytes 10000000 | tf_op jit(solution)/shard_map/last_0/pallas_call | solution.py:288
  303.8 2.1 collective-permute-start.4
  305.8 9.8 %last_1.1.own = bf16[512,896]{1,0:T(8,128)(2,1)} custom-call(s32[1]{0:T(128)} %bitcast.side, bf16[2,2,2048,896]{3,2,1,0:T(8,128)(2,1)} %get-tuple-element.32.late, bf16[1792,896]{1,0:T(8,128)(2,1)} %upstream.1, bf16[2,2,2048,896]{3,2,1,0:T(8,128)(2,1)} %get-tuple-element.36.grad_one, bf16[4096,1792]{1,0:T(8,128)(2,1)} %weights.37), custom_call_target="tpu_custom_call" | custom-call | flops 1644167168 | bytes 10000000 | tf_op jit(solution)/shard_map/last_1/pallas_call | solution.py:288
  315.7 11.5 %collective-permute-done.4.other.refs_0_ = bf16[512,896]{1,0:T(8,128)(2,1)S(1)} collective-permute-done((bf16[512,896]{1,0:T(8,128)(2,1)}, bf16[512,896]{1,0:T(8,128)(2,1)S(1)}, u32[]{:S(2)}, u32[]{:S(2)}) %collective-permute-start.4) | collective-permute-done | bytes 917536 | tf_op jit(solution)/shard_map/ppermute | solution.py:449
  328.1 3.3 outer_update_0.1
  331.5 2.0 collective-permute-start.5
  333.5 9.9 %last_2.1.own = bf16[512,896]{1,0:T(8,128)(2,1)} custom-call(s32[1]{0:T(128)} %bitcast.side, bf16[2,2,2048,896]{3,2,1,0:T(8,128)(2,1)} %get-tuple-element.32.late, bf16[1792,896]{1,0:T(8,128)(2,1)} %upstream.1, bf16[2,2,2048,896]{3,2,1,0:T(8,128)(2,1)} %get-tuple-element.36.grad_one, bf16[4096,1792]{1,0:T(8,128)(2,1)} %weights.37, bf16[512,896]{1,0:T(8,128)(2,1)} %copy-done.10), custom_call_target="tpu_custom_call" | custom-call | flops 1644167168 | bytes 10000000 | tf_op jit(solution)/shard_map/last_2/pallas_call | solution.py:288
  343.4 1.5 collective-permute-start.7
  344.9 2.0 collective-permute-done.3.refs_0_.other
  346.9 1.0 copy-done.8
  347.8 3.3 outer_update_1.1
  351.2 2.0 collective-permute-start.10
  354.1 9.9 %last_3.1.own = bf16[512,896]{1,0:T(8,128)(2,1)} custom-call(s32[1]{0:T(128)} %bitcast.side, bf16[2,2,2048,896]{3,2,1,0:T(8,128)(2,1)} %get-tuple-element.32.late, bf16[1792,896]{1,0:T(8,128)(2,1)} %upstream.1, bf16[2,2,2048,896]{3,2,1,0:T(8,128)(2,1)} %get-tuple-element.36.grad_one, bf16[4096,1792]{1,0:T(8,128)(2,1)} %weights.37, ...), custom_call_target="tpu_custom_call" | custom-call | flops 1644167168 | bytes 10000000 | tf_op jit(solution)/shard_map/last_3/pallas_call | solution.py:288
  364.0 1.5 collective-permute-start.6
  365.5 1.4 collective-permute-done.7.other.refs_0_
  366.9 5.5 %collective-permute-done.10.refs_1_.block = bf16[512,896]{1,0:T(8,128)(2,1)S(1)} collective-permute-done((bf16[512,896]{1,0:T(8,128)(2,1)}, bf16[512,896]{1,0:T(8,128)(2,1)S(1)}, u32[]{:S(2)}, u32[]{:S(2)}) %collective-permute-start.10) | collective-permute-done | bytes 917536 | tf_op jit(solution)/shard_map/ppermute | solution.py:459
  373.3 9.8 %last_4.1.own = bf16[512,896]{1,0:T(8,128)(2,1)} custom-call(s32[1]{0:T(128)} %bitcast.side, bf16[2,2,2048,896]{3,2,1,0:T(8,128)(2,1)} %get-tuple-element.32.late, bf16[1792,896]{1,0:T(8,128)(2,1)} %upstream.1, bf16[2,2,2048,896]{3,2,1,0:T(8,128)(2,1)} %get-tuple-element.36.grad_one, bf16[4096,1792]{1,0:T(8,128)(2,1)} %weights.37, ...), custom_call_target="tpu_custom_call" | custom-call | flops 1644167168 | bytes 10000000 | tf_op jit(solution)/shard_map/last_4/pallas_call | solution.py:288
  383.2 1.4 collective-permute-start.11
  384.6 3.3 outer_update_2.1
  387.9 1.5 collective-permute-start.8
  390.3 3.4 outer_update_3.1
  394.2 10.9 %collective-permute-done.11.other.refs_0_ = bf16[512,896]{1,0:T(8,128)(2,1)S(1)} collective-permute-done((bf16[512,896]{1,0:T(8,128)(2,1)}, bf16[512,896]{1,0:T(8,128)(2,1)S(1)}, u32[]{:S(2)}, u32[]{:S(2)}) %collective-permute-start.11) | collective-permute-done | bytes 917536 | tf_op jit(solution)/shard_map/ppermute | solution.py:449
  406.1 3.3 outer_update_4.1
  409.4 1.7 collective-permute-start.12
  412.4 9.9 %last_5.1.own = bf16[512,896]{1,0:T(8,128)(2,1)} custom-call(s32[1]{0:T(128)} %bitcast.side, bf16[2,2,2048,896]{3,2,1,0:T(8,128)(2,1)} %get-tuple-element.32.late, bf16[1792,896]{1,0:T(8,128)(2,1)} %upstream.1, bf16[2,2,2048,896]{3,2,1,0:T(8,128)(2,1)} %get-tuple-element.36.grad_one, bf16[4096,1792]{1,0:T(8,128)(2,1)} %weights.37, ...), custom_call_target="tpu_custom_call" | custom-call | flops 1644167168 | bytes 10000000 | tf_op jit(solution)/shard_map/last_5/pallas_call | solution.py:288
  422.3 1.2 collective-permute-start.9
  423.5 7.6 %collective-permute-done.14.refs_1_.block = bf16[512,896]{1,0:T(8,128)(2,1)S(1)} collective-permute-done((bf16[512,896]{1,0:T(8,128)(2,1)}, bf16[512,896]{1,0:T(8,128)(2,1)S(1)}, u32[]{:S(2)}, u32[]{:S(2)}) %collective-permute-start.14) | collective-permute-done | bytes 917536 | tf_op jit(solution)/shard_map/ppermute | solution.py:459
  432.0 10.0 %last_6.1.own = bf16[512,896]{1,0:T(8,128)(2,1)} custom-call(s32[1]{0:T(128)} %bitcast.side, bf16[2,2,2048,896]{3,2,1,0:T(8,128)(2,1)} %get-tuple-element.32.late, bf16[1792,896]{1,0:T(8,128)(2,1)} %upstream.1, bf16[2,2,2048,896]{3,2,1,0:T(8,128)(2,1)} %get-tuple-element.36.grad_one, bf16[4096,1792]{1,0:T(8,128)(2,1)} %weights.37, ...), custom_call_target="tpu_custom_call" | custom-call | flops 1644167168 | bytes 10000000 | tf_op jit(solution)/shard_map/last_6/pallas_call | solution.py:288
  442.6 4.0 collective-permute-done.12.refs_1_.block
  448.5 9.9 %last_7.1.own = bf16[512,896]{1,0:T(8,128)(2,1)} custom-call(s32[1]{0:T(128)} %bitcast.side, bf16[2,2,2048,896]{3,2,1,0:T(8,128)(2,1)} %get-tuple-element.32.late, bf16[1792,896]{1,0:T(8,128)(2,1)} %upstream.1, bf16[2,2,2048,896]{3,2,1,0:T(8,128)(2,1)} %get-tuple-element.36.grad_one, bf16[4096,1792]{1,0:T(8,128)(2,1)} %weights.37, ...), custom_call_target="tpu_custom_call" | custom-call | flops 1644167168 | bytes 10000000 | tf_op jit(solution)/shard_map/last_7/pallas_call | solution.py:288
  458.4 1.3 collective-permute-start.13
  459.7 3.3 outer_update_5.1
  463.8 1.7 collective-permute-done.15.other
  465.5 1.0 copy-done.15
  466.5 3.3 outer_update_6.1
  469.8 1.4 collective-permute-start.17
  471.2 11.2 %collective-permute-done.13.other = bf16[512,896]{1,0:T(8,128)(2,1)S(1)} collective-permute-done((bf16[512,896]{1,0:T(8,128)(2,1)}, bf16[512,896]{1,0:T(8,128)(2,1)S(1)}, u32[]{:S(2)}, u32[]{:S(2)}) %collective-permute-start.13) | collective-permute-done | bytes 917536 | tf_op jit(solution)/shard_map/ppermute | solution.py:449
  482.5 1.0 copy-done.16
  483.5 3.3 outer_update_7.1
  487.1 2.2 place_0.1.held
  489.2 2.2 place_1.1.held
  491.4 2.2 place_2.1.held
  493.6 2.2 place_3.1.held
  495.7 2.2 place_4.1.held
  498.9 2.2 place_5.1.held
  501.1 5.1 collective-permute-done.17.block
  507.1 2.2 place_6.1.held
  509.3 11.8 %collective-permute-done.16.block = bf16[512,896]{1,0:T(8,128)(2,1)S(1)} collective-permute-done((bf16[512,896]{1,0:T(8,128)(2,1)}, bf16[512,896]{1,0:T(8,128)(2,1)S(1)}, u32[]{:S(2)}, u32[]{:S(2)}) %collective-permute-start.16) | collective-permute-done | bytes 917536 | tf_op jit(solution)/shard_map/ppermute | solution.py:459
  522.1 2.2 place_7.1
  (50 shorter events, 15.4 us)
Async XLA Ops:
  6.5 83.9 %all-gather.7.cloned.1.call-start = ((), (), s32[]{:S(2)}) async-start(), calls=%async_computation.1 | async-start | bytes 8650752 | tf_op jit(solution)/shard_map/all_gather | solution.py:407
  8.4 169.9 %all-gather.5.cloned.1.call-start = ((), (), s32[]{:S(2)}) async-start(), calls=%async_computation | async-start | bytes 8650752 | tf_op jit(solution)/shard_map/all_gather | solution.py:407
  9.2 4.8 collective-permute-start
  143.7 89.3 %collective-permute-start.1 = (bf16[896,896]{1,0:T(8,128)(2,1)}, bf16[896,896]{1,0:T(8,128)(2,1)S(1)}, u32[]{:S(2)}, u32[]{:S(2)}) collective-permute-start(bf16[896,896]{1,0:T(8,128)(2,1)} %cut_0.1), channel_id=1, source_target_pairs={{0,8},{8,0},{16,24},{24,16},{1,9},{9,1},{17,25},{25,17},{2,10},{10... | collective-permute-start | bytes 4816904 | tf_op jit(solution)/shard_map/ppermute | solution.py:423
  233.0 51.8 %collective-permute-start.2 = (bf16[896,896]{1,0:T(8,128)(2,1)}, bf16[896,896]{1,0:T(8,128)(2,1)S(1)}, u32[]{:S(2)}, u32[]{:S(2)}) collective-permute-start(bf16[896,896]{1,0:T(8,128)(2,1)} %cut_1.1), channel_id=1, source_target_pairs={{0,8},{8,0},{16,24},{24,16},{1,9},{9,1},{17,25},{25,17},{2,10},{10... | collective-permute-start | bytes 4816904 | tf_op jit(solution)/shard_map/ppermute | solution.py:423
  233.0 1.2 copy-start.17
  284.8 1.2 copy-start.11
  303.8 23.4 %collective-permute-start.4 = (bf16[512,896]{1,0:T(8,128)(2,1)}, bf16[512,896]{1,0:T(8,128)(2,1)S(1)}, u32[]{:S(2)}, u32[]{:S(2)}) collective-permute-start(bf16[512,896]{1,0:T(8,128)(2,1)} %last_0.1.own), channel_id=1, source_target_pairs={{0,16},{8,24},{16,0},{24,8},{1,17},{9,25},{17,1},{25,9},{2,18},{10... | collective-permute-start | bytes 2752520 | tf_op jit(solution)/shard_map/ppermute | solution.py:449
  315.7 31.2 %collective-permute-start.3 = (bf16[512,896]{1,0:T(8,128)(2,1)}, bf16[512,896]{1,0:T(8,128)(2,1)S(1)}, u32[]{:S(2)}, u32[]{:S(2)}) collective-permute-start(bf16[512,896]{1,0:T(8,128)(2,1)} %last_1.1.own), channel_id=1, source_target_pairs={{0,16},{8,24},{16,0},{24,8},{1,17},{9,25},{17,1},{25,9},{2,18},{10... | collective-permute-start | bytes 2752520 | tf_op jit(solution)/shard_map/ppermute | solution.py:449
  327.2 0.9 copy-start.10
  331.5 21.7 %collective-permute-start.5 = (bf16[512,896]{1,0:T(8,128)(2,1)}, bf16[512,896]{1,0:T(8,128)(2,1)S(1)}, u32[]{:S(2)}, u32[]{:S(2)}) collective-permute-start(bf16[512,896]{1,0:T(8,128)(2,1)} %get-tuple-element.37), channel_id=1, source_target_pairs={{0,8},{8,0},{16,24},{24,16},{1,9},{9,1},{17,25},{25,17},{2,10},{10... | collective-permute-start | bytes 2752520 | tf_op jit(solution)/shard_map/ppermute | solution.py:459
  343.4 23.5 %collective-permute-start.7 = (bf16[512,896]{1,0:T(8,128)(2,1)}, bf16[512,896]{1,0:T(8,128)(2,1)S(1)}, u32[]{:S(2)}, u32[]{:S(2)}) collective-permute-start(bf16[512,896]{1,0:T(8,128)(2,1)} %last_2.1.own), channel_id=1, source_target_pairs={{0,16},{8,24},{16,0},{24,8},{1,17},{9,25},{17,1},{25,9},{2,18},{10... | collective-permute-start | bytes 2752520 | tf_op jit(solution)/shard_map/ppermute | solution.py:449
  346.9 1.0 copy-start.8
  351.2 21.2 %collective-permute-start.10 = (bf16[512,896]{1,0:T(8,128)(2,1)}, bf16[512,896]{1,0:T(8,128)(2,1)S(1)}, u32[]{:S(2)}, u32[]{:S(2)}) collective-permute-start(bf16[512,896]{1,0:T(8,128)(2,1)} %get-tuple-element.41), channel_id=1, source_target_pairs={{0,8},{8,0},{16,24},{24,16},{1,9},{9,1},{17,25},{25,17},{2,10},{10... | collective-permute-start | bytes 2752520 | tf_op jit(solution)/shard_map/ppermute | solution.py:459
  353.2 0.9 copy-start
  364.0 25.4 %collective-permute-start.6 = (bf16[512,896]{1,0:T(8,128)(2,1)}, bf16[512,896]{1,0:T(8,128)(2,1)S(1)}, u32[]{:S(2)}, u32[]{:S(2)}) collective-permute-start(bf16[512,896]{1,0:T(8,128)(2,1)} %last_3.1.own), channel_id=1, source_target_pairs={{0,16},{8,24},{16,0},{24,8},{1,17},{9,25},{17,1},{25,9},{2,18},{10... | collective-permute-start | bytes 2752520 | tf_op jit(solution)/shard_map/ppermute | solution.py:449
  366.9 5.5 %copy-start.7 = (bf16[512,896]{1,0:T(8,128)(2,1)}, bf16[512,896]{1,0:T(8,128)(2,1)S(1)}, u32[]{:S(2)}) copy-start(bf16[512,896]{1,0:T(8,128)(2,1)S(1)} %collective-permute-done.7.other.refs_0_) | copy-start | bytes 2752516
  372.4 0.9 copy-start.1
  383.2 22.0 %collective-permute-start.11 = (bf16[512,896]{1,0:T(8,128)(2,1)}, bf16[512,896]{1,0:T(8,128)(2,1)S(1)}, u32[]{:S(2)}, u32[]{:S(2)}) collective-permute-start(bf16[512,896]{1,0:T(8,128)(2,1)} %last_4.1.own), channel_id=1, source_target_pairs={{0,16},{8,24},{16,0},{24,8},{1,17},{9,25},{17,1},{25,9},{2,18},{10... | collective-permute-start | bytes 2752520 | tf_op jit(solution)/shard_map/ppermute | solution.py:449
  387.9 23.5 %collective-permute-start.8 = (bf16[512,896]{1,0:T(8,128)(2,1)}, bf16[512,896]{1,0:T(8,128)(2,1)S(1)}, u32[]{:S(2)}, u32[]{:S(2)}) collective-permute-start(bf16[512,896]{1,0:T(8,128)(2,1)} %get-tuple-element.40), channel_id=1, source_target_pairs={{0,8},{8,0},{16,24},{24,16},{1,9},{9,1},{17,25},{25,17},{2,10},{10... | collective-permute-start | bytes 2752520 | tf_op jit(solution)/shard_map/ppermute | solution.py:459
  389.4 0.9 copy-start.5
  393.7 37.4 %collective-permute-start.14 = (bf16[512,896]{1,0:T(8,128)(2,1)}, bf16[512,896]{1,0:T(8,128)(2,1)S(1)}, u32[]{:S(2)}, u32[]{:S(2)}) collective-permute-start(bf16[512,896]{1,0:T(8,128)(2,1)} %get-tuple-element.45), channel_id=1, source_target_pairs={{0,8},{8,0},{16,24},{24,16},{1,9},{9,1},{17,25},{25,17},{2,10},{10... | collective-permute-start | bytes 2752520 | tf_op jit(solution)/shard_map/ppermute | solution.py:459
  405.2 1.0 copy-start.6
  409.4 37.2 %collective-permute-start.12 = (bf16[512,896]{1,0:T(8,128)(2,1)}, bf16[512,896]{1,0:T(8,128)(2,1)S(1)}, u32[]{:S(2)}, u32[]{:S(2)}) collective-permute-start(bf16[512,896]{1,0:T(8,128)(2,1)} %get-tuple-element.44), channel_id=1, source_target_pairs={{0,8},{8,0},{16,24},{24,16},{1,9},{9,1},{17,25},{25,17},{2,10},{10... | collective-permute-start | bytes 2752520 | tf_op jit(solution)/shard_map/ppermute | solution.py:459
  411.4 1.0 copy-start.2
  422.3 24.3 %collective-permute-start.9 = (bf16[512,896]{1,0:T(8,128)(2,1)}, bf16[512,896]{1,0:T(8,128)(2,1)S(1)}, u32[]{:S(2)}, u32[]{:S(2)}) collective-permute-start(bf16[512,896]{1,0:T(8,128)(2,1)} %last_5.1.own), channel_id=1, source_target_pairs={{0,16},{8,24},{16,0},{24,8},{1,17},{9,25},{17,1},{25,9},{2,18},{10... | collective-permute-start | bytes 2752520 | tf_op jit(solution)/shard_map/ppermute | solution.py:449
  431.1 0.9 copy-start.3
  442.0 23.5 %collective-permute-start.15 = (bf16[512,896]{1,0:T(8,128)(2,1)}, bf16[512,896]{1,0:T(8,128)(2,1)S(1)}, u32[]{:S(2)}, u32[]{:S(2)}) collective-permute-start(bf16[512,896]{1,0:T(8,128)(2,1)} %last_6.1.own), channel_id=1, source_target_pairs={{0,16},{8,24},{16,0},{24,8},{1,17},{9,25},{17,1},{25,9},{2,18},{10... | collective-permute-start | bytes 2752520 | tf_op jit(solution)/shard_map/ppermute | solution.py:449
  446.6 1.0 copy-start.4
  447.6 0.9 copy-start.9
  458.4 24.1 %collective-permute-start.13 = (bf16[512,896]{1,0:T(8,128)(2,1)}, bf16[512,896]{1,0:T(8,128)(2,1)S(1)}, u32[]{:S(2)}, u32[]{:S(2)}) collective-permute-start(bf16[512,896]{1,0:T(8,128)(2,1)} %last_7.1.own), channel_id=1, source_target_pairs={{0,16},{8,24},{16,0},{24,8},{1,17},{9,25},{17,1},{25,9},{2,18},{10... | collective-permute-start | bytes 2752520 | tf_op jit(solution)/shard_map/ppermute | solution.py:449
  463.0 34.9 %collective-permute-start.18 = (bf16[512,896]{1,0:T(8,128)(2,1)}, bf16[512,896]{1,0:T(8,128)(2,1)S(1)}, u32[]{:S(2)}, u32[]{:S(2)}) collective-permute-start(bf16[512,896]{1,0:T(8,128)(2,1)} %get-tuple-element.51), channel_id=1, source_target_pairs={{0,8},{8,0},{16,24},{24,16},{1,9},{9,1},{17,25},{25,17},{2,10},{10... | collective-permute-start | bytes 2752520 | tf_op jit(solution)/shard_map/ppermute | solution.py:459
  465.5 1.0 copy-start.15
  469.8 36.3 %collective-permute-start.17 = (bf16[512,896]{1,0:T(8,128)(2,1)}, bf16[512,896]{1,0:T(8,128)(2,1)S(1)}, u32[]{:S(2)}, u32[]{:S(2)}) collective-permute-start(bf16[512,896]{1,0:T(8,128)(2,1)} %get-tuple-element.50), channel_id=1, source_target_pairs={{0,8},{8,0},{16,24},{24,16},{1,9},{9,1},{17,25},{25,17},{2,10},{10... | collective-permute-start | bytes 2752520 | tf_op jit(solution)/shard_map/ppermute | solution.py:459
  482.5 1.0 copy-start.16
  486.8 34.3 %collective-permute-start.16 = (bf16[512,896]{1,0:T(8,128)(2,1)}, bf16[512,896]{1,0:T(8,128)(2,1)S(1)}, u32[]{:S(2)}, u32[]{:S(2)}) collective-permute-start(bf16[512,896]{1,0:T(8,128)(2,1)} %get-tuple-element.49), channel_id=1, source_target_pairs={{0,8},{8,0},{16,24},{24,16},{1,9},{9,1},{17,25},{25,17},{2,10},{10... | collective-permute-start | bytes 2752520 | tf_op jit(solution)/shard_map/ppermute | solution.py:459
  497.9 1.0 copy-start.12
  506.1 1.0 copy-start.13
  521.1 1.0 copy-start.14
Sparse Core Ops, SparseCore 0:
  10.3 80.0 all-gather.6
  93.5 84.7 all-gather.4
